TPU v7x, 256 devices: a whole 4x4x8 slice. The times are simulated.
256 devices in a mesh: dp: 4 (over y_lo, core), blk: 8 (over z), head: 8 (over y_hi, x).
Axes of the slice: x: 4, y: 4 (y_hi: 2, y_lo: 2; y = y_hi * 2 + y_lo), z: 8, core: 2. Of those that a mesh axis runs over, the one named last changes fastest.
Arguments:
- video: bfloat16 [16384, 3072], P(('dp', 'blk'), 'head'), parts along dimension 0, may hold values from -10 to 10
- text: bfloat16 [4096, 3072], P(('dp', 'blk'), 'head'), parts along dimension 0, may hold values from -6 to 6
- shift: float32 [3072], replicated, may hold values from -3 to 3
- scale: float32 [3072], replicated, may hold values from -3 to 3
- gate: float32 [3072], replicated, may hold values from 1 to 6
- w_qkv: bfloat16 [3072, 9216], P('blk', 'head'), may hold values from -1 to 1
- w_out: bfloat16 [3072, 3072], P('head', 'blk'), may hold values from -0.109375 to 0.109375
- q_gain: float32 [128], replicated, may hold values from 1 to 7
- k_gain: float32 [128], replicated, may hold values from 1 to 7
- clip_lengths: int32 [16], P('dp'), parts along dimension 0, may hold values from 1 to 2048, 4096 in all
- text_owner: int32 [16], P('dp'), parts along dimension 0, may hold values from 0 to 3, each once
Outputs:
- video_out: bfloat16 [16384, 3072], P(('dp', 'blk'), 'head'), parts along dimension 0
- text_out: bfloat16 [4096, 3072], P(('dp', 'blk'), 'head'), parts along dimension 0
There are 4 independent parts, one for each index of `dp`. A program takes and returns all parts, laid end to end along the dimension named above; an argument that names none is the same for every part. Nothing has to cross between parts.
Inputs may be any that keep to these rules, and one draw needn't show every extreme that they name: `clip_lengths`: the clip lengths sum to 4096; the longest is exactly 2048. `text_owner`: each clip owns exactly one block of text rows.
All inputs are finite; a program needn't handle non-finite values.
Results may differ from a plain program's by a relative error of at most 0.018.
The roundings to bfloat16 on the way count: a program that leaves them out, or rounds other values in their place, can miss the bound.
Values may be sent and summed in bfloat16 or wider, within the bound.
A program may use at most 128 MiB of HBM per device.

v0:
```python
import jax
import jax.numpy as jnp
from jax import lax
from jax.sharding import PartitionSpec as P

TXT = 256


def rotate(values, angles):
    half = values.shape[-1] // 2
    cosine = jnp.cos(angles)[:, None, :]
    sine = jnp.sin(angles)[:, None, :]
    first = values[..., :half]
    second = values[..., half:]
    return jnp.concatenate(
        [first * cosine - second * sine, second * cosine + first * sine], axis=-1
    )


def rms_scale(values, gain):
    return values * lax.rsqrt(jnp.mean(values * values, axis=-1, keepdims=True) + 1e-06) * gain


def lookup(indices, table):
    slots = jnp.arange(table.shape[0], dtype=jnp.int32)
    return jnp.sum(jnp.where(indices[:, None] == slots[None, :], table[None, :], 0), axis=1)


def video_clip_of(indices, ends):
    return jnp.sum((indices[:, None] >= ends[None, :]).astype(jnp.int32), axis=1)


def text_clip_of(indices, owners):
    return lookup(indices // TXT, owners)


def mixed_clip_of(first_row, count, video_rows, text_rows, ends, owners):
    shard_rows = video_rows + text_rows
    row_index = first_row + jnp.arange(count, dtype=jnp.int32)
    shard_id = row_index // shard_rows
    offset = row_index - shard_id * shard_rows
    video_part = offset < video_rows
    video_ids = video_clip_of(shard_id * video_rows + offset, ends)
    text_ids = text_clip_of(jnp.maximum(shard_id * text_rows + offset - video_rows, 0), owners)
    return jnp.where(video_part, video_ids, text_ids)


def absorb(carry, key_part, value_part, key_clip, queries, query_clip, factor):
    best, totals, summed = carry
    scores = (
        jnp.einsum("qhd,khd->hqk", queries, key_part, preferred_element_type=jnp.float32) * factor
    )
    allowed = (query_clip[:, None] == key_clip[None, :])[None]
    scores = jnp.where(allowed, scores, -1e30)
    newest = jnp.maximum(best, jnp.max(scores, axis=-1))
    weights = jnp.where(allowed, jnp.exp(scores - newest[..., None]), 0.0)
    totals = jnp.sum(weights, axis=-1)
    summed = jnp.einsum(
        "hqk,khd->hqd", weights.astype(jnp.bfloat16), value_part, preferred_element_type=jnp.float32
    )
    return (newest, totals, summed)


def guarded(carry, key_part, value_part, key_clip, queries, query_clip, factor):
    return absorb(carry, key_part, value_part, key_clip, queries, query_clip, factor)


def on_device(
    video, text, shift, scale, gate, w_qkv, w_out, q_gain, k_gain, clip_lengths, text_owner
):
    video_rows = video.shape[0]
    text_rows = text.shape[0]
    shard_rows = video_rows + text_rows
    local_width = video.shape[1]
    head_size = q_gain.shape[0]
    local_heads = w_qkv.shape[1] // (3 * head_size)
    block_index = lax.axis_index("blk")
    head_index = lax.axis_index("head")
    ends = jnp.cumsum(clip_lengths)
    starts = ends - clip_lengths
    local_tokens = jnp.concatenate([video, text], axis=0)
    whole = lax.all_gather(local_tokens, "head", axis=1, tiled=True)
    as_float = whole.astype(jnp.float32)
    mean = jnp.mean(as_float, axis=1, keepdims=True)
    var = jnp.mean((as_float - mean) ** 2, axis=1, keepdims=True)
    modulated = ((as_float - mean) * lax.rsqrt(var + 1e-06) * (1.0 + scale) + shift).astype(
        jnp.bfloat16
    )
    qkv = jnp.dot(
        modulated,
        lax.all_gather(w_qkv, "blk", axis=0, tiled=True),
        preferred_element_type=jnp.float32,
    )
    qkv = qkv.reshape(shard_rows, local_heads, 3, head_size)
    query_clip = mixed_clip_of(
        block_index * shard_rows, shard_rows, video_rows, text_rows, ends, text_owner
    )
    video_index = block_index * video_rows + jnp.arange(video_rows, dtype=jnp.int32)
    video_ids = video_clip_of(video_index, ends)
    video_place = (video_index - lookup(video_ids, starts)).astype(jnp.float32)
    places = jnp.concatenate([video_place, jnp.zeros((text_rows,), jnp.float32)])
    is_video = jnp.arange(shard_rows, dtype=jnp.int32) < video_rows
    freqs = 10000.0 ** (-2.0 * jnp.arange(head_size // 2, dtype=jnp.float32) / head_size)
    angles = places[:, None] * freqs[None, :]
    queries = rms_scale(qkv[:, :, 0], q_gain)
    keys = rms_scale(qkv[:, :, 1], k_gain)
    queries = jnp.where(is_video[:, None, None], rotate(queries, angles), queries).astype(
        jnp.bfloat16
    )
    keys = jnp.where(is_video[:, None, None], rotate(keys, angles), keys).astype(jnp.bfloat16)
    values = qkv[:, :, 2].astype(jnp.bfloat16)
    factor = 1.0 / head_size**0.5
    start_state = (
        jnp.full((local_heads, shard_rows), -1e30, jnp.float32),
        jnp.zeros((local_heads, shard_rows), jnp.float32),
        jnp.zeros((local_heads, shard_rows, head_size), jnp.float32),
    )
    pieces = (
        lax.all_gather(keys, "blk", axis=0, tiled=True),
        lax.all_gather(values, "blk", axis=0, tiled=True),
    )
    key_clip = mixed_clip_of(
        jnp.int32(0), pieces[0].shape[0], video_rows, text_rows, ends, text_owner
    )
    final_state = guarded(start_state, pieces[0], pieces[1], key_clip, queries, query_clip, factor)
    summed = final_state[2] / final_state[1][..., None]
    attended = (
        summed.transpose(1, 0, 2).reshape(shard_rows, local_heads * head_size).astype(jnp.bfloat16)
    )
    partial_sums = jnp.dot(
        attended,
        lax.all_gather(w_out, "blk", axis=1, tiled=True),
        preferred_element_type=jnp.float32,
    )
    projected = lax.psum_scatter(
        partial_sums.astype(jnp.bfloat16), "head", scatter_dimension=1, tiled=True
    ).astype(jnp.float32)
    gate_here = lax.dynamic_slice_in_dim(gate, head_index * local_width, local_width)
    updated = (local_tokens.astype(jnp.float32) + gate_here * projected).astype(jnp.bfloat16)
    return (updated[:video_rows], updated[video_rows:])


def solution(mesh):
    return jax.shard_map(
        on_device,
        mesh=mesh,
        in_specs=(
            P(("dp", "blk"), "head"),
            P(("dp", "blk"), "head"),
            P(),
            P(),
            P(),
            P("blk", "head"),
            P("head", "blk"),
            P(),
            P(),
            P("dp"),
            P("dp"),
        ),
        out_specs=(P(("dp", "blk"), "head"), P(("dp", "blk"), "head")),
        check_vma=False,
    )
```

profile of v0, /device:TPU:32, one launch (start us, length us, event | category | flops | bytes accessed | tf_op | source)
XLA Modules:
  0.0 451.6 jit_solution(371458791362755740)
XLA Ops:
  7.2 1.0 constant_dynamic-update-slice_fusion.1
  8.3 0.9 constant_dynamic-update-slice_fusion
  9.2 0.8 copy-done.1
  10.0 0.0 all-gather.9.cloned.1.call-start
  10.0 0.7 all-gather.9.cloned.1.call-update
  10.8 0.8 reduce-window.8
  11.6 0.1 convert_reduce_fusion.3
  11.7 0.7 bitcast_subtract_fusion
  12.4 0.1 select_reduce_fusion.2
  12.5 0.7 broadcast_add_fusion
  13.2 2.0 multiply_cosine_fusion
  15.2 78.5 %all-gather.7.cloned.1.call-done = bf16[640,3072]{1,0:T(8,128)(2,1)} async-done(((bf16[640,384]{1,0:T(8,128)(2,1)}), bf16[640,3072]{1,0:T(8,128)(2,1)}) %all-gather.7.cloned.1.call-update) | async-done | bytes 3932176 | tf_op jit(solution)/shard_map/all_gather | solution.py:82
  93.7 2.7 convert_reduce_fusion
  96.4 3.3 fusion.8
  99.7 74.8 %all-gather.9.cloned.1.call-done = bf16[3072,1152]{1,0:T(8,128)(2,1)} async-done(((bf16[384,1152]{1,0:T(8,128)(2,1)}), bf16[3072,1152]{1,0:T(8,128)(2,1)}) %all-gather.9.cloned.1.call-update) | async-done | bytes 7077904 | tf_op jit(solution)/shard_map/all_gather | solution.py:91
  174.5 10.7 %fusion.12 = f32[640,1152]{0,1:T(8,128)S(1)} fusion(bf16[3072,1152]{1,0:T(8,128)(2,1)} %all-gather.9.cloned.1.call-done, bf16[640,3072]{1,0:T(8,128)(2,1)} %all-gather.7.cloned.1.call-done, f32[3072]{0:T(1024)S(1)} %copy-done.7, f32[3072]{0:T(1024)S(1)} %broadcast_add_fusion, f32[640]{0:T(1024)S(1)} %add_rsqrt_fusion.2, f32[640]{0:T(1024)S(1)} %broadcast_multiply_fusion), kind=kOutput, calls=%fused_computation.17 | convolution fusion | flops 4541644800 | bytes 13988864 | tf_op jit(solution)/shard_map/dot_general | solution.py:89
  185.2 0.1 fusion.57
  185.4 1.4 copy-done.3
  186.8 0.3 copy.32
  187.1 0.4 fusion.36
  187.5 0.3 copy.31
  187.8 0.4 fusion.38
  188.2 0.6 fusion.37
  188.8 0.9 copy-done
  189.8 2.6 multiply_subtract_fusion.1
  192.4 1.1 fusion.35
  193.5 0.0 all-gather.15.cloned.1.call-start
  193.6 1.3 slice.43
  194.9 0.8 copy.35
  195.8 0.5 all-gather.13.cloned.1.call-update
  196.4 0.1 convert_reduce_fusion.2
  196.5 0.1 select_reduce_fusion.1
  196.6 0.2 select_reduce_fusion
  196.8 1.9 broadcast_compare_fusion
  198.7 45.9 %all-gather.11.cloned.1.call-done = bf16[5120,3,128]{2,0,1:T(8,128)(2,1)} async-done(((bf16[640,3,128]{2,0,1:T(8,128)(2,1)}), bf16[5120,3,128]{2,0,1:T(8,128)(2,1)}) %all-gather.11.cloned.1.call-update) | async-done | bytes 3932176 | tf_op jit(solution)/shard_map/all_gather | solution.py:119
  244.7 19.5 %fusion = (f32[3,640]{1,0:T(4,128)S(1)}, f32[3,640,5120]{2,1,0:T(8,128)}) fusion(pred[640,5120]{1,0:T(8,128)(4,1)S(1)} %broadcast_compare_fusion, bf16[5120,3,128]{2,0,1:T(8,128)(2,1)} %all-gather.11.cloned.1.call-done, f32[640,3,128]{2,0,1:T(8,128)} %copy-done, bf16[640,3,64]{2,0,1:T(8,128)(2,1)} %get-tuple-element.5, ...), kind=kOutput, calls=%fused_computation.2 | convolution fusion | flops 2547300352 | bytes 48013440 | tf_op jit(solution)/shard_map/qhd,khd->hqk/dot_general | solution.py:51
  264.1 19.0 %fusion.1 = f32[3,640]{1,0:T(4,128)S(1)} fusion(f32[3,640,5120]{2,1,0:T(8,128)} %get-tuple-element.13, f32[3,640]{1,0:T(4,128)S(1)} %broadcast_maximum_fusion, pred[640,5120]{1,0:T(8,128)(4,1)S(1)} %broadcast_compare_fusion), kind=kLoop, calls=%fused_computation.3 | loop fusion | flops 49150080 | bytes 42613760 | tf_op jit(solution)/shard_map/reduce_sum | solution.py:57
  283.1 14.2 %all-gather.15.cloned.1.call-done = bf16[5120,3,1,128]{0,3,1,2:T(8,128)(2,1)} async-done(((bf16[640,3,1,128]{0,3,1,2:T(8,128)(2,1)}), bf16[5120,3,1,128]{0,3,1,2:T(8,128)(2,1)}) %all-gather.15.cloned.1.call-update) | async-done | bytes 3932176 | tf_op jit(solution)/shard_map/all_gather | solution.py:120
  297.3 19.1 %fusion.29 = bf16[640,3,128]{0,2,1:T(8,128)(2,1)} fusion(bf16[5120,3,1,128]{0,3,1,2:T(8,128)(2,1)} %all-gather.15.cloned.1.call-done, f32[3,640,5120]{2,1,0:T(8,128)} %get-tuple-element.13, f32[3,640]{1,0:T(4,128)S(1)} %broadcast_maximum_fusion, pred[640,5120]{1,0:T(8,128)(4,1)S(1)} %broadcast_compare_fusion, f32[640,3]{0,1:T(4,128)S(1)} %bitcast.45), kind=kOutput, calls=%fused_computation.25 | convolution fusion | flops 2566225920 | bytes 47037440 | tf_op jit(solution)/shard_map/hqk,khd->hqd/dot_general | solution.py:58
  316.4 25.1 %all-gather.13.cloned.1.call-done = bf16[384,3072]{1,0:T(8,128)(2,1)} async-done(((bf16[384,384]{1,0:T(8,128)(2,1)}), bf16[384,3072]{1,0:T(8,128)(2,1)}) %all-gather.13.cloned.1.call-update) | async-done | bytes 2359312 | tf_op jit(solution)/shard_map/all_gather | solution.py:132
  341.5 5.9 %convolution_convert_fusion = bf16[640,3072]{1,0:T(8,128)(2,1)} fusion(bf16[640,384]{0,1:T(8,128)(2,1)} %bitcast.50, bf16[384,3072]{1,0:T(8,128)(2,1)} %all-gather.13.cloned.1.call-done), kind=kOutput, calls=%fused_computation.16 | convolution fusion | flops 1511915520 | bytes 6782976 | tf_op jit(solution)/shard_map/dot_general | solution.py:130
  347.5 6.1 %copy.29 = bf16[640,3072]{0,1:T(8,128)(2,1)} copy(bf16[640,3072]{1,0:T(8,128)(2,1)} %convolution_convert_fusion) | data formatting | bytes 7864320
  353.6 0.8 dynamic_slice.3
  354.4 87.5 %reduce-scatter.4.cloned.1.call-done = bf16[384,640]{1,0:T(8,128)(2,1)} async-done(((bf16[3072,640]{1,0:T(8,128)(2,1)}), bf16[384,640]{1,0:T(8,128)(2,1)}) %reduce-scatter.4.cloned.1.call-update) | async-done | bytes 491536
  441.9 1.3 copy.30
  443.2 0.2 add_convert_fusion
  443.3 0.8 slice.44
  444.1 0.7 slice.45
  (36 shorter events, 0.4 us)
Async XLA Ops:
  7.2 167.3 %copy-start.7 = (f32[3072]{0:T(1024)S(1)}, f32[3072]{0:T(1024)}, u32[]{:S(2)}) copy-start(f32[3072]{0:T(1024)} %param.13) | copy-start | bytes 36868
  7.2 86.6 %all-gather.7.cloned.1.call-start = ((), (), s32[]{:S(2)}) async-start(), calls=%async_computation.1 | async-start | bytes 4423680 | tf_op jit(solution)/shard_map/all_gather | solution.py:82
  9.2 0.8 copy-start.1
  10.0 164.5 %all-gather.9.cloned.1.call-start = ((), (), s32[]{:S(2)}) async-start(), calls=%async_computation.2 | async-start | bytes 7962624 | tf_op jit(solution)/shard_map/all_gather | solution.py:91
  10.8 233.9 %all-gather.11.cloned.1.call-start = ((), (), s32[]{:S(2)}) async-start(), calls=%async_computation.3 | async-start | bytes 4423680 | tf_op jit(solution)/shard_map/all_gather | solution.py:119
  185.2 1.6 copy-start.3
  185.2 3.0 copy-start.5
  185.2 3.0 copy-start.6
  188.2 8.3 %copy-start.4 = (s32[4]{0:T(128)S(1)}, s32[4]{0:T(128)}, u32[]{:S(2)}) copy-start(s32[4]{0:T(128)} %param.21) | copy-start | bytes 52
  188.8 1.0 copy-start
  193.5 103.8 %all-gather.15.cloned.1.call-start = ((), (), s32[]{:S(2)}) async-start(), calls=%async_computation.5 | async-start | bytes 4423680 | tf_op jit(solution)/shard_map/all_gather | solution.py:120
  195.7 145.8 %all-gather.13.cloned.1.call-start = ((), (), s32[]{:S(2)}) async-start(), calls=%async_computation.4 | async-start | bytes 2654208 | tf_op jit(solution)/shard_map/all_gather | solution.py:132
  196.3 245.6 %reduce-scatter.4.cloned.1.call-start = ((), (), s32[]{:S(2)}) async-start(), calls=%async_computation.6 | async-start | bytes 4423680
  347.5 95.7 %copy-start.2 = (bf16[640,384]{1,0:T(8,128)(2,1)S(1)}, bf16[640,384]{1,0:T(8,128)(2,1)}, u32[]{:S(2)}) copy-start(bf16[640,384]{1,0:T(8,128)(2,1)} %copy-done.1) | copy-start | bytes 1474564
Sparse Core Ops, SparseCore 0:
  10.5 83.2 all-gather.6
  95.5 78.9 all-gather.8
  193.7 50.9 all-gather.10
  246.3 50.9 all-gather.14
  299.0 42.5 all-gather.12
  353.7 88.0 reduce-scatter.3
where the time goes:
time: 452 us
  waiting for transfers between devices  327 us (72%)
  matrix products  55.2 us (12%)
  other arithmetic  36.9 us (8%)
  local copies, waits for them, and re-layouts  17.6 us (4%)
  between operations  14.3 us (3%)
    unnamed x7, waiting for transfers between devices  88.8 us
    all_gather x1, waiting for transfers between devices, on_device(): whole = lax.all_gather(local_tokens, 'head', axis=1, tiled=True)  78.5 us
    all_gather x1, waiting for transfers between devices, on_device(): lax.all_gather(w_qkv, 'blk', axis=0, tiled=True)  74.8 us
    all_gather x1, waiting for transfers between devices, on_device(): lax.all_gather(keys, 'blk', axis=0, tiled=True)  45.9 us
    all_gather x1, waiting for transfers between devices, on_device(): lax.all_gather(w_out, 'blk', axis=1, tiled=True)  25.1 us
    dot_general x1, matrix products, absorb(): jnp.einsum('qhd,khd->hqk', queries, key_part, preferred_element_type=jnp....  19.5 us
    dot_general x1, matrix products, absorb(): jnp.einsum('hqk,khd->hqd', weights.astype(jnp.bfloat16), value_part, pref...  19.1 us
    reduce_sum x1, other arithmetic, absorb(): totals = jnp.sum(weights, axis=-1)  19 us
  transfers between devices with their start and end apart: 6, of which 6 were waited for; matrix products, arithmetic and copies ran while one was open for 16% of the time, Pallas kernels for 0%

commit v1 on v0

v1 whole, which is shorter than its diff:
```python
import functools
import math

import jax
import jax.numpy as jnp
import numpy as np
from jax import lax
from jax.experimental import pallas as pl
from jax.experimental.pallas import tpu as pltpu
from jax.sharding import PartitionSpec as P

MESH = pl.DeviceIdType.MESH
BF = jnp.bfloat16
F32 = jnp.float32
ROWS = 640
VROWS = 512
WIDTH = 384
HD = 128
TILE = 128
TXT = 256


def remote(src, dst, send_sem, recv_sem, device):
    return pltpu.make_async_remote_copy(
        src_ref=src,
        dst_ref=dst,
        send_sem=send_sem,
        recv_sem=recv_sem,
        device_id=device,
        device_id_type=MESH,
    )


def greet(devices):
    barrier = pltpu.get_barrier_semaphore()
    for device in devices:
        pl.semaphore_signal(barrier, inc=1, device_id=device, device_id_type=MESH)
    pl.semaphore_wait(barrier, len(devices))


def project_kernel(
    video,
    text,
    w_qkv,
    w_out,
    shift,
    scale,
    q_gain,
    k_gain,
    freqs,
    lengths,
    q_out,
    kv_out,
    wo_out,
    tok,
    mod,
    wbuf,
    ring,
    wo,
    cos_t,
    sin_t,
    local_sem,
    tok_recv,
    tok_send,
    left_recv,
    right_recv,
    right_send,
    left_send,
    sib_recv,
    sib_send,
    swap_recv,
    swap_send,
    pair_recv,
    pair_send,
):
    dp, z, head = lax.axis_index("dp"), lax.axis_index("blk"), lax.axis_index("head")
    core = lax.rem(dp, 2)
    yh, x = head // 4, lax.rem(head, 4)
    sibling = (dp + 1 - 2 * core, z, head)
    up, down = (dp, lax.rem(z + 1, 8), head), (dp, lax.rem(z + 7, 8), head)
    xs = [lax.rem(x + d, 4) for d in range(4)]
    slot = [[yh * 4 + xs[d] for d in range(4)], [(1 - yh) * 4 + xs[d] for d in range(4)]]
    right, left, over = (dp, z, slot[0][1]), (dp, z, slot[0][3]), (dp, z, slot[1][0])
    greet([(dp, z, lax.rem(head + d, 8)) for d in range(1, 8)] + [up, down, sibling])

    sends = []

    def send(copy):
        copy.start()
        sends.append(copy)

    def cols_of(h):
        return pl.ds(pl.multiple_of(h * WIDTH, WIDTH), WIDTH)

    def tok_at(h, t, half=None):
        first, count = t * TILE, TILE
        if half is not None:
            first, count = first + half * (TILE // 2), TILE // 2
        return tok.at[pl.ds(first, count), cols_of(h)]

    def own_tile(t):
        return video.at[pl.ds(t * TILE, TILE)] if t < 4 else text.at[pl.ds(0, TILE)]

    def tok_sem(flip, dx, t, half):
        return tok_recv.at[flip, dx, t, half]

    send_count = [0]

    def tok_copy(src, h, t, half, flip, dx, device):
        index = send_count[0]
        send_count[0] += 1
        send(
            remote(
                src,
                tok_at(h, t, half),
                tok_send.at[index],
                tok_sem(flip, dx, t, half or 0),
                device,
            )
        )

    def tok_wait(flip, dx, t, half=None):
        ref = tok_at(slot[flip][dx], t, half)
        pltpu.make_async_copy(ref, ref, tok_sem(flip, dx, t, half or 0)).wait()

    def w_at(block, p, half=None):
        if p >= 6:
            first, count = (0, 64) if half is None else (half * 32, 32)
            return ring.at[block, p - 6, pl.ds(first, count)]
        first, count = (0, 192) if half is None else (half * 96, 96)
        rows = pl.ds(pl.multiple_of(block * WIDTH + core * 192 + first, 32), count)
        return wbuf.at[rows, w_cols(p)]

    def w_cols(p):
        return pl.ds(384 * p + 128, 256) if p < 3 else pl.ds(384 * (p - 3), 128)

    def own_piece(p):
        if p >= 6:
            return w_out.at[pl.ds(pl.multiple_of((p - 6) * 128 + core * 64, 64), 64)]
        return w_qkv.at[pl.ds(pl.multiple_of(core * 192, 192), 192), w_cols(p)]

    def ring_first(p):
        send(remote(own_piece(p), w_at(z, p), right_send.at[p, 0], left_recv.at[p, 0], up))
        send(remote(own_piece(p), w_at(z, p), left_send.at[p, 0], right_recv.at[p, 0], down))

    def swap(block, p):
        hh = p - 6
        target = wo.at[hh, head, core]

        @pl.when(block != head)
        def _():
            remote(
                ring.at[block, hh],
                target,
                swap_send.at[hh, block],
                swap_recv.at[hh, head],
                (dp, z, block),
            ).start()

        @pl.when(block == head)
        def _():
            pltpu.make_async_copy(ring.at[block, hh], target, swap_recv.at[hh, head]).start()

    def ring_step(p, s):
        lo, hi = lax.rem(z + 8 - s, 8), lax.rem(z + s, 8)
        half_a, half_b = (0, 1) if s == 4 else (None, None)
        ref = w_at(lo, p, half_a)
        pltpu.make_async_copy(ref, ref, left_recv.at[p, s - 1]).wait()
        if s < 4:
            src = w_at(lo, p, 0 if s == 3 else None)
            send(remote(src, src, right_send.at[p, s], left_recv.at[p, s], up))
        ref = w_at(hi, p, half_b)
        pltpu.make_async_copy(ref, ref, right_recv.at[p, s - 1]).wait()
        if s < 4:
            src = w_at(hi, p, 1 if s == 3 else None)
            send(remote(src, src, left_send.at[p, s], right_recv.at[p, s], down))
        if p < 6:
            for i, (block, half) in enumerate(((lo, half_a), (hi, half_b))):
                ref = w_at(block, p, half)
                k = 2 * (s - 1) + i
                send(remote(ref, ref, sib_send.at[p, k], sib_recv.at[p, k], sibling))
        elif s < 4:
            swap(lo, p)
            swap(hi, p)
        else:
            swap(lo, p)

    def sib_wait(p):
        for s in range(1, 5):
            for i in range(2):
                count = 96 if s == 4 else 192
                block = lax.rem(z + 8 - s, 8) if i == 0 else lax.rem(z + s, 8)
                first = i * 96 if s == 4 else 0
                rows = pl.ds(
                    pl.multiple_of(block * WIDTH + (1 - core) * 192 + first, 32), count
                )
                ref = wbuf.at[rows, w_cols(p)]
                pltpu.make_async_copy(ref, ref, sib_recv.at[p, 2 * (s - 1) + i]).wait()

    own = [
        pltpu.make_async_copy(video, tok.at[pl.ds(0, VROWS), cols_of(head)], local_sem.at[0]),
        pltpu.make_async_copy(
            text, tok.at[pl.ds(VROWS, ROWS - VROWS), cols_of(head)], local_sem.at[1]
        ),
        pltpu.make_async_copy(
            w_qkv, wbuf.at[pl.ds(pl.multiple_of(z * WIDTH, WIDTH), WIDTH)], local_sem.at[2]
        ),
    ] + [
        pltpu.make_async_copy(own_piece(p), w_at(z, p), local_sem.at[3 + p - 6]) for p in (6, 7, 8)
    ]
    for p in range(3):
        ring_first(p)
    for t in range(5):
        tok_copy(own_tile(t), head, t, None, 1, 0, over)
        tok_copy(own_tile(t), head, t, None, 0, 3, right)
        tok_copy(own_tile(t), head, t, None, 0, 1, left)
    for copy in own:
        copy.start()

    e0 = lengths[0]
    e1 = e0 + lengths[1]
    e2 = e1 + lengths[2]
    row = lax.broadcasted_iota(jnp.int32, (ROWS, HD), 0)
    place = z * VROWS + row
    start = jnp.where(place >= e0, e0, 0)
    start = jnp.where(place >= e1, e1, start)
    start = jnp.where(place >= e2, e2, start)
    place = jnp.where(row < VROWS, place - start, 0).astype(F32)
    angle = place * freqs[...]
    lane = lax.broadcasted_iota(jnp.int32, (ROWS, HD), 1)

    def wait_x1(t):
        for dx, half, device, far in ((3, 0, right, 2), (1, 1, left, 2)):
            tok_wait(0, dx, t)
            h = slot[0][dx]
            tok_copy(tok_at(h, t, half), h, t, half, 0, far, device)
            if t >= 3:
                tok_copy(tok_at(h, t), h, t, None, 1, dx, over)

    for t in range(3):
        tok_wait(1, 0, t)
        h = slot[1][0]
        tok_copy(tok_at(h, t), h, t, None, 1, 3, right)
        tok_copy(tok_at(h, t), h, t, None, 1, 1, left)
        ring_step(t, 1)
    cos_t[...] = jnp.cos(angle)
    sin_t[...] = jnp.where(lane < HD // 2, -jnp.sin(angle), jnp.sin(angle))
    for t in range(5):
        wait_x1(t)
        if t >= 2:
            ring_step(t - 2, 2)
    for t in range(3):
        for dx, half, device in ((3, 0, right), (1, 1, left)):
            tok_wait(1, dx, t)
            h = slot[1][dx]
            tok_copy(tok_at(h, t, half), h, t, half, 1, 2, device)
        ring_step(t, 3)
    for p in range(3, 9):
        ring_first(p)
    for t in (3, 4, 0, 1, 2):
        for half in range(2):
            tok_wait(0, 2, t, half)
        if t >= 3:
            h = slot[0][2]
            for half in range(2):
                tok_copy(tok_at(h, t, half), h, t, half, 1, 2, over)
        if t < 3:
            ring_step(t, 4)
    for p in range(3, 9):
        ring_step(p, 1)
    for t in range(3):
        for half in range(2):
            tok_wait(1, 2, t, half)
    for t in (3, 4):
        tok_wait(1, 0, t)
        tok_wait(1, 1, t)
        tok_wait(1, 3, t)
        for half in range(2):
            tok_wait(1, 2, t, half)
    for copy in own:
        copy.wait()
    for p in (6, 7, 8):
        swap(z, p)

    def normalise(first, count):
        @pl.loop(0, count)
        def _(i):
            rows = pl.ds(pl.multiple_of(first + i * 16, 16), 16)
            value = tok[rows, :].astype(F32)
            mean = jnp.sum(value, axis=1, keepdims=True) * (1.0 / 3072.0)
            value = value - mean
            var = jnp.sum(value * value, axis=1, keepdims=True) * (1.0 / 3072.0)
            value = value * lax.rsqrt(var + 1e-06) * (1.0 + scale[...]) + shift[...]
            mod[rows, :] = value.astype(BF)

    def rms_rope(value, gain):
        mean = jnp.sum(value * value, axis=1, keepdims=True) * (1.0 / HD)
        value = value * lax.rsqrt(mean + 1e-06) * gain
        return value * cos_t[...] + pltpu.roll(value, HD // 2, 1) * sin_t[...]

    normalise(0, 40)
    for p in range(3, 9):
        ring_step(p, 2)
    for p in range(3):
        sib_wait(p)

    @pl.loop(0, 3)
    def _(h):
        cols = pl.ds(pl.multiple_of(h * 384 + 128, 128), 256)
        kv = jnp.dot(mod[...], wbuf[:, cols], preferred_element_type=F32)
        kv_out[h, :, 0:HD] = rms_rope(kv[:, 0:HD], k_gain[...]).astype(BF)
        kv_out[h, :, HD : 2 * HD] = kv[:, HD : 2 * HD].astype(BF)

    for s in (3, 4):
        for p in range(3, 9):
            ring_step(p, s)
    for p in range(3, 6):
        sib_wait(p)

    for hh in range(3):
        for d in range(8):
            src = lax.rem(head + d, 8)
            ref = wo.at[hh, src, core]
            pltpu.make_async_copy(ref, ref, swap_recv.at[hh, src]).wait()
        ref = wo.at[hh, :, core]
        send(remote(ref, ref, pair_send.at[hh], pair_recv.at[hh], sibling))

    @pl.loop(0, 3)
    def _(h):
        cols = pl.ds(pl.multiple_of(h * 384, 128), 128)
        q = jnp.dot(mod[...], wbuf[:, cols], preferred_element_type=F32)
        q_out[h] = rms_rope(q, q_gain[...]).astype(BF)

    for hh in range(3):
        ref = wo.at[hh, :, 1 - core]
        pltpu.make_async_copy(ref, ref, pair_recv.at[hh]).wait()
    done = pltpu.make_async_copy(wo, wo_out, local_sem.at[6])
    done.start()
    for hh in range(3):
        for d in range(1, 8):
            block = lax.rem(head + d, 8)
            remote(
                ring.at[block, hh],
                wo.at[hh, head, core],
                swap_send.at[hh, block],
                swap_recv.at[hh, head],
                (dp, z, block),
            ).wait_send()
    for copy in sends:
        copy.wait_send()
    done.wait()


def attend_kernel(
    q,
    kv_in,
    wo,
    video,
    text,
    gate,
    lengths,
    owners,
    video_out,
    text_out,
    kvbuf,
    att,
    proj,
    best,
    total,
    acc,
    q_clip,
    local_sem,
    left_recv,
    right_recv,
    right_send,
    left_send,
    att_recv,
    att_send,
):
    dp, z, head = lax.axis_index("dp"), lax.axis_index("blk"), lax.axis_index("head")
    up, down = (dp, lax.rem(z + 1, 8), head), (dp, lax.rem(z + 7, 8), head)
    peers = [(dp, z, lax.rem(head + d, 8)) for d in range(1, 8)]
    greet(peers + [up, down])

    def own_sends(h):
        for i in range(2):
            remote(
                kv_in.at[h, i], kvbuf.at[h, z, i], right_send.at[h, i], left_recv.at[h, i], up
            ).start()
            remote(
                kv_in.at[h, 1 - i],
                kvbuf.at[h, z, 1 - i],
                left_send.at[h, i],
                right_recv.at[h, i],
                down,
            ).start()

    own_sends(0)
    own = pltpu.make_async_copy(kv_in, kvbuf.at[:, z], local_sem.at[0])
    own.start()

    e0 = lengths[0]
    e1 = e0 + lengths[1]
    e2 = e1 + lengths[2]

    def clips(place, is_video, owner):
        ids = (
            (place >= e0).astype(jnp.int32)
            + (place >= e1).astype(jnp.int32)
            + (place >= e2).astype(jnp.int32)
        )
        return jnp.where(is_video, ids, owner)

    row = lax.broadcasted_iota(jnp.int32, (ROWS, HD), 0)
    q_clip[...] = clips(z * VROWS + row, row < VROWS, owners[z // 2])
    proj[...] = jnp.zeros_like(proj)

    factor = math.log2(math.e) / math.sqrt(HD)

    def unit(h, b, first):
        keys = kvbuf[h, b, :, :, 0:HD].reshape(ROWS, HD)
        values = kvbuf[h, b, :, :, HD : 2 * HD].reshape(ROWS, HD)
        column = lax.broadcasted_iota(jnp.int32, (1, ROWS), 1)
        key_clip = clips(b * VROWS + column, column < VROWS, owners[b // 2])
        for t in range(5):
            rows = pl.ds(t * TILE, TILE)
            scores = lax.dot_general(
                q[h, rows, :], keys, (((1,), (1,)), ((), ())), preferred_element_type=F32
            )
            scores = jnp.where(q_clip[rows, 0:1] == key_clip, scores, -1e30)
            old = jnp.where(first, -1e30, best[rows, 0:1])
            newest = jnp.maximum(old, jnp.max(scores, axis=1, keepdims=True))
            weights = jnp.exp2((scores - newest) * factor)
            keep = jnp.exp2((old - newest) * factor)
            best[rows, :] = jnp.broadcast_to(newest, (TILE, HD))
            count = jnp.sum(weights, axis=1, keepdims=True)
            summed = jnp.dot(weights.astype(BF), values, preferred_element_type=F32)
            prior = jnp.where(first, 0.0, total[rows, 0:1])
            before = jnp.where(first, 0.0, acc[rows, :])
            total[rows, :] = jnp.broadcast_to(prior * keep + count, (TILE, HD))
            acc[rows, :] = before * keep + summed

    mine = pl.ds(pl.multiple_of(head * HD, HD), HD)

    def att_copy(h, d):
        part = att.at[h, :, mine]
        return remote(part, part, att_send.at[h, d], att_recv.at[h, 8 - d], peers[d - 1])

    def finish(h):
        att[h, :, mine] = (acc[...] / total[...]).astype(BF)
        for d in range(1, 8):
            att_copy(h, d).start()

    def out_project(h):
        for d in range(1, 8):
            src = lax.rem(head + d, 8)
            ref = att.at[h, :, pl.ds(pl.multiple_of(src * HD, HD), HD)]
            pltpu.make_async_copy(ref, ref, att_recv.at[h, d]).wait()
        proj[...] += jnp.dot(att[h], wo[h].reshape(8 * HD, WIDTH), preferred_element_type=F32)

    own.wait()

    def slot(t, carry):
        h, j = t // 7, lax.rem(t, 7)
        odd = lax.rem(j, 2)
        lo, hi = lax.rem(z + 7 - j // 2, 8), lax.rem(z + 1 + j // 2, 8)
        from_left, from_right = kvbuf.at[h, lo, odd], kvbuf.at[h, hi, 1 - odd]
        pltpu.make_async_copy(from_left, from_left, left_recv.at[h, j]).wait()

        @pl.when(j < 5)
        def _():
            remote(
                from_left, from_left, right_send.at[h, j + 2], left_recv.at[h, j + 2], up
            ).start()

        pltpu.make_async_copy(from_right, from_right, right_recv.at[h, j]).wait()

        @pl.when(j < 5)
        def _():
            remote(
                from_right, from_right, left_send.at[h, j + 2], right_recv.at[h, j + 2], down
            ).start()

        @pl.when((j == 4) & (h < 2))
        def _():
            own_sends(h + 1)

        @pl.when((j == 0) & (h > 0))
        def _():
            unit(h - 1, lax.rem(z + 4, 8), False)
            finish(h - 1)

        away = (j + 1) // 2
        unit(h, lax.rem(jnp.where(odd == 1, z + 8 - away, z + away), 8), j == 0)

        @pl.when((j == 5) & (h > 0))
        def _():
            out_project(h - 1)

        return carry

    lax.fori_loop(0, 21, slot, 0)
    unit(2, lax.rem(z + 4, 8), False)
    finish(2)
    out_project(2)
    scaled = gate[...] * proj[...]
    video_out[...] = (video[...].astype(F32) + scaled[0:VROWS]).astype(BF)
    text_out[...] = (text[...].astype(F32) + scaled[VROWS:ROWS]).astype(BF)

    def drain(t, carry):
        h, j = t // 7, lax.rem(t, 7)
        remote(
            kvbuf.at[h, z, 0], kvbuf.at[h, z, 0], right_send.at[h, j], left_recv.at[h, j], up
        ).wait_send()
        remote(
            kvbuf.at[h, z, 0], kvbuf.at[h, z, 0], left_send.at[h, j], right_recv.at[h, j], down
        ).wait_send()
        return carry

    lax.fori_loop(0, 21, drain, 0)
    for h in range(3):
        for d in range(1, 8):
            att_copy(h, d).wait_send()


def on_device(
    video, text, shift, scale, gate, w_qkv, w_out, q_gain, k_gain, clip_lengths, text_owner
):
    anywhere = pl.BlockSpec(memory_space=pl.ANY)
    vmem = pl.BlockSpec(memory_space=pltpu.VMEM)
    smem = pl.BlockSpec(memory_space=pltpu.SMEM)
    dma = pltpu.SemaphoreType.DMA
    exponents = np.arange(HD // 2, dtype=np.float64) * (-2.0 / HD)
    freqs = np.tile((10000.0**exponents).astype(np.float32), 2).reshape(1, HD)
    queries, key_values, wo = pl.pallas_call(
        project_kernel,
        name="project",
        out_shape=(
            jax.ShapeDtypeStruct((3, ROWS, HD), BF),
            jax.ShapeDtypeStruct((3, ROWS, 2 * HD), BF),
            jax.ShapeDtypeStruct((3, 8, 2, 64, WIDTH), BF),
        ),
        in_specs=[anywhere] * 4 + [vmem] * 5 + [smem],
        out_specs=(vmem, vmem, anywhere),
        scratch_shapes=[
            pltpu.VMEM((ROWS, 3072), BF),
            pltpu.VMEM((ROWS, 3072), BF),
            pltpu.VMEM((3072, 1152), BF),
            pltpu.VMEM((8, 3, 64, WIDTH), BF),
            pltpu.VMEM((3, 8, 2, 64, WIDTH), BF),
            pltpu.VMEM((ROWS, HD), F32),
            pltpu.VMEM((ROWS, HD), F32),
            dma((7,)),
            dma((2, 4, 5, 2)),
            dma((64,)),
            dma((9, 4)),
            dma((9, 4)),
            dma((9, 4)),
            dma((9, 4)),
            dma((6, 8)),
            dma((6, 8)),
            dma((3, 8)),
            dma((3, 8)),
            dma((3,)),
            dma((3,)),
        ],
        compiler_params=pltpu.CompilerParams(
            collective_id=1, has_side_effects=True, vmem_limit_bytes=52 * 2**20
        ),
    )(
        video,
        text,
        w_qkv,
        w_out,
        shift.reshape(1, -1),
        scale.reshape(1, -1),
        q_gain.reshape(1, HD),
        k_gain.reshape(1, HD),
        jnp.asarray(freqs),
        clip_lengths,
    )
    gate_here = lax.dynamic_slice_in_dim(gate, lax.axis_index("head") * WIDTH, WIDTH)
    return pl.pallas_call(
        attend_kernel,
        name="attend",
        out_shape=(
            jax.ShapeDtypeStruct((VROWS, WIDTH), BF),
            jax.ShapeDtypeStruct((ROWS - VROWS, WIDTH), BF),
        ),
        in_specs=[vmem, anywhere, vmem, vmem, vmem, vmem, smem, smem],
        out_specs=(vmem, vmem),
        scratch_shapes=[
            pltpu.VMEM((3, 8, 2, ROWS // 2, 2 * HD), BF),
            pltpu.VMEM((3, ROWS, 8 * HD), BF),
            pltpu.VMEM((ROWS, WIDTH), F32),
            pltpu.VMEM((ROWS, HD), F32),
            pltpu.VMEM((ROWS, HD), F32),
            pltpu.VMEM((ROWS, HD), F32),
            pltpu.VMEM((ROWS, HD), jnp.int32),
            dma((1,)),
            dma((3, 7)),
            dma((3, 7)),
            dma((3, 7)),
            dma((3, 7)),
            dma((3, 8)),
            dma((3, 8)),
        ],
        compiler_params=pltpu.CompilerParams(
            collective_id=2, has_side_effects=True, vmem_limit_bytes=52 * 2**20
        ),
    )(
        queries,
        key_values.reshape(3, 2, ROWS // 2, 2 * HD),
        wo,
        video,
        text,
        gate_here.reshape(1, WIDTH),
        clip_lengths,
        text_owner,
    )


def solution(mesh):
    return jax.shard_map(
        on_device,
        mesh=mesh,
        in_specs=(
            P(("dp", "blk"), "head"),
            P(("dp", "blk"), "head"),
            P(),
            P(),
            P(),
            P("blk", "head"),
            P("head", "blk"),
            P(),
            P(),
            P("dp"),
            P("dp"),
        ),
        out_specs=(P(("dp", "blk"), "head"), P(("dp", "blk"), "head")),
        check_vma=False,
    )
```

time: 452 us -> 200 us (0.44)
  waiting for transfers between devices: 327 us -> 0 us
  Pallas kernels: 0 us -> 187 us
  matrix products: 55.2 us -> 0 us
  other arithmetic: 36.9 us -> 0 us
  between operations: 14.3 us -> 0.67 us
  local copies, waits for them, and re-layouts: 17.6 us -> 9.7 us
    all_gather x5 -> x0, waiting for transfers between devices: 239 us -> none  [the longest x1 78.5 us: on_device(): whole = lax.all_gather(local_tokens, 'head', axis=1, tiled=True)]
    pallas_call x0 -> x2, Pallas kernels: none -> 187 us  [the longest x1 113 us: on_device(): pl.pallas_call(attend_kernel, name='attend', out_shape=(jax.ShapeDtypeStr...]
    unnamed x7 -> x0, waiting for transfers between devices: 88.8 us -> none
    dot_general x4 -> x0, matrix products: 55.2 us -> none  [the longest x1 19.5 us: absorb(): jnp.einsum('qhd,khd->hqk', queries, key_part, preferred_element_type=jnp....]
    reduce_sum x10 -> x0, other arithmetic: 26.2 us -> none  [the longest x1 19 us: absorb(): totals = jnp.sum(weights, axis=-1)]
  transfers between devices with their start and end apart: 6 -> 0, of which waited for: 6 -> 0; matrix products, arithmetic and copies ran while one was open for 16% -> 0% of each run, Pallas kernels for 0% -> 0%
where the time goes in v1:
time: 200 us; the launch traced here: 198 us
  Pallas kernels  187 us (94%)
  local copies, waits for them, and re-layouts  9.7 us (5%)
    pallas_call x1, Pallas kernels, on_device(): pl.pallas_call(attend_kernel, name='attend', out_shape=(jax.ShapeDtypeStr...  113 us
    pallas_call x1, Pallas kernels, on_device(): pl.pallas_call(project_kernel, name='project', out_shape=(jax.ShapeDtypeS...  74.7 us
    unnamed x22, local copies, waits for them, and re-layouts  8.92 us

profile of v1, /device:TPU:32, one launch (start us, length us, event | category | flops | bytes accessed | tf_op | source)
XLA Modules:
  0.0 197.7 jit_solution(12087187673112442896)
XLA Ops:
  0.6 0.8 dynamic_slice.3
  1.4 0.0 copy-start
  1.4 1.0 copy-done
  2.4 0.0 copy-start.1
  2.4 0.9 copy-done.1
  3.3 0.0 copy-start.2
  3.3 1.0 copy-done.2
  4.3 0.0 copy-start.3
  4.3 0.7 copy-done.3
  5.0 0.0 copy-start.4
  5.0 0.7 copy-done.4
  5.7 0.0 copy-start.5
  5.7 0.7 copy-done.5
  6.3 0.0 copy-start.6
  6.3 0.7 copy-done.6
  7.0 0.0 copy-start.7
  7.0 0.7 copy-done.7
  7.7 0.0 copy-start.8
  7.7 0.7 copy-done.8
  8.3 74.7 %project.1 = (bf16[3,640,128]{2,1,0:T(8,128)(2,1)S(1)}, bf16[3,640,256]{2,1,0:T(8,128)(2,1)}, bf16[3,8,2,64,384]{4,3,2,1,0:T(8,128)(2,1)}) custom-call(bf16[512,384]{1,0:T(8,128)(2,1)S(1)} %copy-done, bf16[128,384]{1,0:T(8,128)(2,1)S(1)} %copy-done.1, bf16[384,1152]{1,0:T(8,128)(2,1)} %w_qkv.1, bf16[384,384]{1,0:T(8,128)(2,1)S(1)} %copy-done.2, ...), custom_call_target="tpu_custom_call" | custom-call | tf_op jit(solution)/shard_map/project/pallas_call | solution.py:535
  83.0 0.0 copy-start.9
  83.1 0.6 copy-done.9
  83.7 112.6 %attend.1 = (bf16[512,384]{1,0:T(8,128)(2,1)S(1)}, bf16[128,384]{1,0:T(8,128)(2,1)S(1)}) custom-call(bf16[3,640,128]{2,1,0:T(8,128)(2,1)S(1)} %get-tuple-element.5.q, bf16[3,2,320,256]{3,2,1,0:T(8,128)(2,1)} %bitcast.9, bf16[3,8,2,64,384]{4,3,2,1,0:T(8,128)(2,1)} %get-tuple-element.7.wo, bf16[512,384]{1,0:T(8,128)(2,1)S(1)} %copy-done, ...), custom_call_target="tpu_custom_call" | custom-call | tf_op jit(solution)/shard_map/attend/pallas_call | solution.py:583
  196.3 0.7 copy.16
  197.0 0.6 copy.17
  (1 shorter events, 0.0 us)
Async XLA Ops:
  1.4 1.0 copy-start
  2.4 0.9 copy-start.1
  3.3 1.0 copy-start.2
  4.3 0.7 copy-start.3
  5.0 0.7 copy-start.4
  5.7 0.7 copy-start.5
  6.3 0.7 copy-start.6
  7.0 0.7 copy-start.7
  7.7 0.7 copy-start.8
  83.0 0.7 copy-start.9

commit v2 on v0

v2 whole, which is shorter than its diff:
```python
import functools
import math

import jax
import jax.numpy as jnp
import numpy as np
from jax import lax
from jax.experimental import pallas as pl
from jax.experimental.pallas import tpu as pltpu
from jax.sharding import PartitionSpec as P

MESH = pl.DeviceIdType.MESH
BF = jnp.bfloat16
F32 = jnp.float32
ROWS = 640
VROWS = 512
WIDTH = 384
HD = 128
TILE = 128


def remote(src, dst, send_sem, recv_sem, device):
    return pltpu.make_async_remote_copy(
        src_ref=src,
        dst_ref=dst,
        send_sem=send_sem,
        recv_sem=recv_sem,
        device_id=device,
        device_id_type=MESH,
    )


def greet(devices):
    barrier = pltpu.get_barrier_semaphore()
    for device in devices:
        pl.semaphore_signal(barrier, inc=1, device_id=device, device_id_type=MESH)
    pl.semaphore_wait(barrier, len(devices))


PARTS = {"all": (0, 128, 0), "a": (0, 64, 0), "b": (64, 64, 1), "a0": (0, 32, 0), "a1": (32, 32, 2)}


def sublayer_kernel(
    video,
    text,
    w_qkv,
    w_out,
    shift_in,
    scale_in,
    gate_in,
    q_gain_in,
    k_gain_in,
    freqs_in,
    lengths,
    owners,
    video_out,
    text_out,
    tok,
    mod,
    wkv,
    wq,
    ring,
    wo,
    cos_t,
    sin_t,
    shift,
    scale,
    gate,
    q_gain,
    k_gain,
    freqs,
    q,
    kvbuf,
    att,
    proj,
    best,
    total,
    acc,
    q_clip,
    local_sem,
    tok_recv,
    tok_send,
    wl_recv,
    wr_recv,
    wr_send,
    wl_send,
    sib_recv,
    sib_send,
    ol_recv,
    or_recv,
    or_send,
    ol_send,
    swap_recv,
    swap_send,
    share_recv,
    share_send,
    left_recv,
    right_recv,
    right_send,
    left_send,
    att_recv,
    att_send,
    last_recv,
    last_send,
):
    dp, z, head = lax.axis_index("dp"), lax.axis_index("blk"), lax.axis_index("head")
    core = lax.rem(dp, 2)
    yh, x = head // 4, lax.rem(head, 4)
    sibling = (dp + 1 - 2 * core, z, head)
    mates = [sibling] + [
        (d, z, head) for d in (lax.rem(dp + 2, 4), lax.rem(dp + 2, 4) + 1 - 2 * core)
    ]
    up, down = (dp, lax.rem(z + 1, 8), head), (dp, lax.rem(z + 7, 8), head)
    xs = [lax.rem(x + d, 4) for d in range(4)]
    slot = [[yh * 4 + xs[d] for d in range(4)], [(1 - yh) * 4 + xs[d] for d in range(4)]]
    right, left, over = (dp, z, slot[0][1]), (dp, z, slot[0][3]), (dp, z, slot[1][0])
    peers = [(dp, z, lax.rem(head + d, 8)) for d in range(1, 8)]
    greet(peers + [up, down] + mates)

    sends = []

    def send(copy):
        copy.start()
        sends.append(copy)

    def landed(ref, sem):
        pltpu.make_async_copy(ref, ref, sem).wait()

    def cols_of(h):
        return pl.ds(pl.multiple_of(h * WIDTH, WIDTH), WIDTH)

    def tok_at(h, t, part):
        first, count, _ = PARTS[part]
        return tok.at[pl.ds(t * TILE + first, count), cols_of(h)]

    def own_tile(t):
        return video.at[pl.ds(t * TILE, TILE)] if t < 4 else text.at[pl.ds(0, TILE)]

    send_count = [0]

    def tok_copy(src, h, t, part, flip, dx, device):
        index = send_count[0]
        send_count[0] += 1
        arrival = tok_recv.at[flip, dx, t, PARTS[part][2]]
        send(remote(src, tok_at(h, t, part), tok_send.at[index], arrival, device))

    def tok_pass(h, t, part, flip, dx, device):
        tok_copy(tok_at(h, t, part), h, t, part, flip, dx, device)

    def tok_wait(flip, dx, t, part):
        landed(tok_at(slot[flip][dx], t, part), tok_recv.at[flip, dx, t, PARTS[part][2]])

    def stage0(t):
        tok_copy(own_tile(t), head, t, "all", 0, 3, right)
        tok_copy(own_tile(t), head, t, "all", 0, 1, left)
        tok_copy(own_tile(t), head, t, "all", 1, 0, over)

    def stage1(t):
        tok_wait(1, 0, t, "all")
        tok_pass(slot[1][0], t, "a", 1, 3, right)
        tok_pass(slot[1][0], t, "a", 1, 1, left)
        for dx, part, device in ((3, "a", right), (1, "b", left)):
            tok_wait(0, dx, t, "all")
            tok_pass(slot[0][dx], t, part, 0, 2, device)
            tok_pass(slot[0][dx], t, "b", 1, dx, over)

    def stage2(t):
        for dx, part, device in ((3, "a0", right), (1, "a1", left)):
            tok_wait(1, dx, t, "a")
            tok_pass(slot[1][dx], t, part, 1, 2, device)
        tok_wait(0, 2, t, "a")
        tok_wait(0, 2, t, "b")
        tok_pass(slot[0][2], t, "b", 1, 2, over)

    def stage3(t):
        for dx, part in ((2, "a0"), (2, "a1"), (1, "b"), (3, "b"), (2, "b")):
            tok_wait(1, dx, t, part)
        normalise(t)

    def normalise(t):
        @pl.loop(0, 8)
        def _(i):
            rows = pl.ds(pl.multiple_of(t * TILE + i * 16, 16), 16)
            value = tok[rows, :].astype(F32)
            mean = jnp.sum(value, axis=1, keepdims=True) * (1.0 / 3072.0)
            value = value - mean
            var = jnp.sum(value * value, axis=1, keepdims=True) * (1.0 / 3072.0)
            value = value * lax.rsqrt(var + 1e-06) * (1.0 + scale[...]) + shift[...]
            mod[rows, :] = value.astype(BF)

    def w_at(block, p, half=None, side=None):
        first, count = (0, 192) if half is None else (half * 96, 96)
        side = core if side is None else side
        rows = pl.ds(pl.multiple_of(block * WIDTH + side * 192 + first, 32), count)
        return wkv.at[rows, pl.ds(256 * p, 256)] if p < 3 else wq.at[rows, pl.ds(128 * p - 384, 128)]

    def w_cols(p):
        return pl.ds(384 * p + 128, 256) if p < 3 else pl.ds(384 * (p - 3), 128)

    def ring_first(p):
        src = w_qkv.at[pl.ds(pl.multiple_of(core * 192, 192), 192), w_cols(p)]
        send(remote(src, w_at(z, p), wr_send.at[p, 0], wl_recv.at[p, 0], up))
        send(remote(src, w_at(z, p), wl_send.at[p, 0], wr_recv.at[p, 0], down))

    def ring_step(p, s):
        lo, hi = lax.rem(z + 8 - s, 8), lax.rem(z + s, 8)
        half_a, half_b = (0, 1) if s == 4 else (None, None)
        landed(w_at(lo, p, half_a), wl_recv.at[p, s - 1])
        if s < 4:
            src = w_at(lo, p, 0 if s == 3 else None)
            send(remote(src, src, wr_send.at[p, s], wl_recv.at[p, s], up))
        landed(w_at(hi, p, half_b), wr_recv.at[p, s - 1])
        if s < 4:
            src = w_at(hi, p, 1 if s == 3 else None)
            send(remote(src, src, wl_send.at[p, s], wr_recv.at[p, s], down))
        for i, (block, half) in enumerate(((lo, half_a), (hi, half_b))):
            ref = w_at(block, p, half)
            k = 2 * (s - 1) + i
            send(remote(ref, ref, sib_send.at[p, k], sib_recv.at[p, k], sibling))

    def sib_wait(p):
        for s in range(1, 5):
            for i in range(2):
                block = lax.rem(z + 8 - s, 8) if i == 0 else lax.rem(z + s, 8)
                ref = w_at(block, p, i if s == 4 else None, 1 - core)
                landed(ref, sib_recv.at[p, 2 * (s - 1) + i])

    quarter = w_out.at[:, pl.ds(pl.multiple_of(dp * 32, 32), 32)]

    def out_first():
        send(remote(quarter, ring.at[z], or_send.at[0], ol_recv.at[0], up))
        send(remote(quarter, ring.at[z], ol_send.at[0], or_recv.at[0], down))

    def out_at(block, half):
        return ring.at[block] if half is None else ring.at[block, :, pl.ds(half * 16, 16)]

    def out_sends(s):
        lo, hi = lax.rem(z + 8 - s, 8), lax.rem(z + s, 8)
        a, b = out_at(lo, 0 if s == 3 else None), out_at(hi, 1 if s == 3 else None)
        return (
            remote(a, a, or_send.at[s], ol_recv.at[s], up),
            remote(b, b, ol_send.at[s], or_recv.at[s], down),
        )

    def out_step(s):
        lo, hi = lax.rem(z + 8 - s, 8), lax.rem(z + s, 8)
        landed(out_at(lo, 0 if s == 4 else None), ol_recv.at[s - 1])
        landed(out_at(hi, 1 if s == 4 else None), or_recv.at[s - 1])
        if s < 4:
            for copy in out_sends(s):
                send(copy)

    def swap_copy(d):
        block = lax.rem(head + d, 8)
        target = wo.at[:, head, dp]
        return remote(
            ring.at[block], target, swap_send.at[d], swap_recv.at[8 - d], (dp, z, block)
        )

    swap_own = pltpu.make_async_copy(ring.at[head], wo.at[:, head, dp], swap_recv.at[0])

    def swap():
        for d in range(1, 8):
            swap_copy(d).start()
        swap_own.start()

    def share_copy(i):
        part = wo.at[:, :, mates[1][0] if i == 2 else dp]
        return remote(part, part, share_send.at[i], share_recv.at[i], mates[i % 2])

    def share():
        for d in range(8):
            landed(wo.at[:, lax.rem(head + d, 8), dp], swap_recv.at[d])
        for i in range(2):
            share_copy(i).start()

    def share_on():
        landed(wo.at[:, :, mates[1][0]], share_recv.at[1])
        share_copy(2).start()

    def share_wait():
        landed(wo.at[:, :, mates[0][0]], share_recv.at[0])
        landed(wo.at[:, :, mates[2][0]], share_recv.at[2])

    own = [
        pltpu.make_async_copy(video, tok.at[pl.ds(0, VROWS), cols_of(head)], local_sem.at[0]),
        pltpu.make_async_copy(
            text, tok.at[pl.ds(VROWS, ROWS - VROWS), cols_of(head)], local_sem.at[1]
        ),
        pltpu.make_async_copy(quarter, ring.at[z], local_sem.at[2]),
    ]
    block_rows = pl.ds(pl.multiple_of(z * WIDTH, WIDTH), WIDTH)
    for p in range(6):
        target = wkv.at[:, pl.ds(256 * p, 256)] if p < 3 else wq.at[:, pl.ds(128 * p - 384, 128)]
        own.append(
            pltpu.make_async_copy(
                w_qkv.at[:, w_cols(p)], target.at[block_rows], local_sem.at[3 + p]
            )
        )
    small = [
        pltpu.make_async_copy(a, b, local_sem.at[9 + i])
        for i, (a, b) in enumerate(
            (
                (freqs_in, freqs),
                (shift_in, shift),
                (scale_in, scale),
                (q_gain_in, q_gain),
                (k_gain_in, k_gain),
                (gate_in.at[:, cols_of(head)], gate),
            )
        )
    ]
    for p in range(6):
        ring_first(p)
    out_first()
    for t in range(3):
        stage0(t)
    for copy in small + own:
        copy.start()
    for copy in small:
        copy.wait()

    e0 = lengths[0]
    e1 = e0 + lengths[1]
    e2 = e1 + lengths[2]

    def clips(place, is_video, owner):
        ids = (
            (place >= e0).astype(jnp.int32)
            + (place >= e1).astype(jnp.int32)
            + (place >= e2).astype(jnp.int32)
        )
        return jnp.where(is_video, ids, owner)

    def tables(t):
        rows = pl.ds(t * TILE, TILE)
        row = lax.broadcasted_iota(jnp.int32, (TILE, HD), 0) + t * TILE
        place = z * VROWS + row
        q_clip[rows, :] = clips(place, row < VROWS, owners[z // 2])
        start = jnp.where(place >= e0, e0, 0)
        start = jnp.where(place >= e1, e1, start)
        start = jnp.where(place >= e2, e2, start)
        place = jnp.where(row < VROWS, place - start, 0).astype(F32)
        angle = place * freqs[...]
        lane = lax.broadcasted_iota(jnp.int32, (TILE, HD), 1)
        sine = jnp.sin(angle)
        cos_t[rows, :] = jnp.cos(angle)
        sin_t[rows, :] = jnp.where(lane < HD // 2, -sine, sine)

    def rms_rope(value, gain):
        mean = jnp.sum(value * value, axis=1, keepdims=True) * (1.0 / HD)
        value = value * lax.rsqrt(mean + 1e-06) * gain
        return value * cos_t[...] + pltpu.roll(value, HD // 2, 1) * sin_t[...]

    def ring_steps(s, *pieces):
        for p in pieces:
            if p == 6:
                out_step(s)
            else:
                ring_step(p, s)

    tables(0)
    stage1(0)
    stage0(3)
    ring_steps(1, 0, 1)
    tables(1)
    stage1(1)
    stage2(0)
    stage0(4)
    ring_steps(1, 2, 3)
    tables(2)
    for copy in own:
        copy.wait()
    stage1(2)
    stage2(1)
    ring_steps(1, 4, 5, 6)
    stage3(0)
    tables(3)
    stage1(3)
    stage2(2)
    ring_steps(2, 0, 1, 2)
    stage3(1)
    tables(4)
    stage1(4)
    stage2(3)
    ring_steps(2, 3, 4, 5, 6)
    stage3(2)
    stage2(4)
    ring_steps(3, 0, 1, 2)
    stage3(3)
    ring_steps(3, 3, 4, 5, 6)
    stage3(4)
    ring_steps(4, 0, 1, 2)
    sib_wait(0)

    def own_sends(h):
        for i in range(2):
            a, b = kvbuf.at[h, z, i], kvbuf.at[h, z, 1 - i]
            remote(a, a, right_send.at[h, i], left_recv.at[h, i], up).start()
            remote(b, b, left_send.at[h, i], right_recv.at[h, i], down).start()

    def pass_on(h, j):
        odd = lax.rem(j, 2)
        lo, hi = lax.rem(z + 7 - j // 2, 8), lax.rem(z + 1 + j // 2, 8)
        from_left, from_right = kvbuf.at[h, lo, odd], kvbuf.at[h, hi, 1 - odd]
        landed(from_left, left_recv.at[h, j])

        @pl.when(j < 5)
        def _():
            remote(
                from_left, from_left, right_send.at[h, j + 2], left_recv.at[h, j + 2], up
            ).start()

        landed(from_right, right_recv.at[h, j])

        @pl.when(j < 5)
        def _():
            remote(
                from_right, from_right, left_send.at[h, j + 2], right_recv.at[h, j + 2], down
            ).start()

    for h in range(3):
        kv = jnp.dot(mod[...], wkv[:, 256 * h : 256 * h + 256], preferred_element_type=F32)
        keys = rms_rope(kv[:, 0:HD], k_gain[...]).astype(BF)
        values = kv[:, HD : 2 * HD].astype(BF)
        for i in range(2):
            rows = slice(i * (ROWS // 2), (i + 1) * (ROWS // 2))
            kvbuf[h, z, i, :, 0:HD] = keys[rows]
            kvbuf[h, z, i, :, HD : 2 * HD] = values[rows]
        if h == 0:
            own_sends(0)
            ring_steps(4, 3, 4, 5, 6)
            swap()
            sib_wait(1)
            sib_wait(2)
        else:
            pass_on(0, h - 1)
    for p in range(3, 6):
        sib_wait(p)
    queries = jnp.dot(mod[...], wq[...], preferred_element_type=F32)
    for h in range(3):
        q[h] = rms_rope(queries[:, h * HD : (h + 1) * HD], q_gain[...]).astype(BF)
    proj[...] = jnp.zeros_like(proj)

    factor = math.log2(math.e) / math.sqrt(HD)
    mine = pl.ds(pl.multiple_of(head * HD, HD), HD)

    def unit(h, b, first, each=None):
        keys = kvbuf[h, b, :, :, 0:HD].reshape(ROWS, HD)
        values = kvbuf[h, b, :, :, HD : 2 * HD].reshape(ROWS, HD)
        column = lax.broadcasted_iota(jnp.int32, (1, ROWS), 1)
        key_clip = clips(b * VROWS + column, column < VROWS, owners[b // 2])
        for t in range(5):
            rows = pl.ds(t * TILE, TILE)
            scores = lax.dot_general(
                q[h, rows, :], keys, (((1,), (1,)), ((), ())), preferred_element_type=F32
            )
            scores = jnp.where(q_clip[rows, 0:1] == key_clip, scores, -1e30)
            old = jnp.where(first, -1e30, best[rows, 0:1])
            newest = jnp.maximum(old, jnp.max(scores, axis=1, keepdims=True))
            weights = jnp.exp2((scores - newest) * factor)
            keep = jnp.exp2((old - newest) * factor)
            best[rows, :] = jnp.broadcast_to(newest, (TILE, HD))
            count = jnp.sum(weights, axis=1, keepdims=True)
            summed = jnp.dot(weights.astype(BF), values, preferred_element_type=F32)
            prior = jnp.where(first, 0.0, total[rows, 0:1])
            before = jnp.where(first, 0.0, acc[rows, :])
            total[rows, :] = jnp.broadcast_to(prior * keep + count, (TILE, HD))
            acc[rows, :] = before * keep + summed
            if each is not None:
                each(t)

    def att_copy(h, d):
        part = att.at[h, :, mine]
        return remote(part, part, att_send.at[h, d], att_recv.at[h, 8 - d], peers[d - 1])

    def finish(h):
        att[h, :, mine] = (acc[...] / total[...]).astype(BF)
        for d in range(1, 8):
            att_copy(h, d).start()

    def from_peer(d):
        return pl.ds(pl.multiple_of(lax.rem(head + d, 8) * HD, HD), HD)

    def out_project(h):
        for d in range(1, 8):
            landed(att.at[h, :, from_peer(d)], att_recv.at[h, d])
        proj[...] += jnp.dot(att[h], wo[h].reshape(8 * HD, WIDTH), preferred_element_type=F32)

    def last_copy(t, d):
        part = att.at[2, pl.ds(t * TILE, TILE), mine]
        return remote(part, part, last_send.at[t, d], last_recv.at[t, 8 - d], peers[d - 1])

    def finish_tile(t):
        rows = pl.ds(t * TILE, TILE)
        att[2, rows, mine] = (acc[rows, :] / total[rows, :]).astype(BF)
        for d in range(1, 8):
            last_copy(t, d).start()

    def step(t, carry):
        h, j = t // 7, lax.rem(t, 7)
        odd = lax.rem(j, 2)

        @pl.when(t >= 2)
        def _():
            pass_on(h, j)

        @pl.when((j == 1) & (h < 2))
        def _():
            own_sends(h + 1)

        @pl.when(t == 1)
        def _():
            share()

        @pl.when(t == 8)
        def _():
            share_on()

        @pl.when((j == 0) & (h > 0))
        def _():
            unit(h - 1, lax.rem(z + 4, 8), False)
            finish(h - 1)

        away = (j + 1) // 2
        unit(h, lax.rem(jnp.where(odd == 1, z + 8 - away, z + away), 8), j == 0)

        @pl.when(t == 17)
        def _():
            share_wait()
            out_project(0)

        @pl.when(t == 19)
        def _():
            out_project(1)

        return carry

    lax.fori_loop(0, 21, step, 0)
    unit(2, lax.rem(z + 4, 8), False, finish_tile)
    weights_out = wo[2].reshape(8 * HD, WIDTH)
    for t in range(5):
        rows = pl.ds(t * TILE, TILE)
        for d in range(1, 8):
            landed(att.at[2, rows, from_peer(d)], last_recv.at[t, d])
        summed = proj[rows, :] + jnp.dot(att[2, rows, :], weights_out, preferred_element_type=F32)
        residual = tok[rows, cols_of(head)].astype(F32)
        result = (residual + gate[...] * summed).astype(BF)
        if t < 4:
            video_out[rows, :] = result
        else:
            text_out[...] = result

    def drain(t, carry):
        h, j = t // 7, lax.rem(t, 7)
        part = kvbuf.at[h, z, 0]
        remote(part, part, right_send.at[h, j], left_recv.at[h, j], up).wait_send()
        remote(part, part, left_send.at[h, j], right_recv.at[h, j], down).wait_send()
        return carry

    lax.fori_loop(0, 21, drain, 0)
    for d in range(1, 8):
        swap_copy(d).wait_send()
        for h in range(2):
            att_copy(h, d).wait_send()
        for t in range(5):
            last_copy(t, d).wait_send()
    for i in range(3):
        share_copy(i).wait_send()
    for copy in sends:
        copy.wait_send()


def on_device(
    video, text, shift, scale, gate, w_qkv, w_out, q_gain, k_gain, clip_lengths, text_owner
):
    anywhere = pl.BlockSpec(memory_space=pl.ANY)
    vmem = pl.BlockSpec(memory_space=pltpu.VMEM)
    smem = pl.BlockSpec(memory_space=pltpu.SMEM)
    dma = pltpu.SemaphoreType.DMA
    exponents = np.arange(HD // 2, dtype=np.float64) * (-2.0 / HD)
    freqs = np.tile((10000.0**exponents).astype(np.float32), 2).reshape(1, HD)
    return pl.pallas_call(
        sublayer_kernel,
        name="sublayer",
        out_shape=(
            jax.ShapeDtypeStruct((VROWS, WIDTH), BF),
            jax.ShapeDtypeStruct((ROWS - VROWS, WIDTH), BF),
        ),
        in_specs=[anywhere] * 10 + [smem] * 2,
        out_specs=(vmem, vmem),
        scratch_shapes=[
            pltpu.VMEM((ROWS, 3072), BF),
            pltpu.VMEM((ROWS, 3072), BF),
            pltpu.VMEM((3072, 768), BF),
            pltpu.VMEM((3072, 384), BF),
            pltpu.VMEM((8, 3, 32, WIDTH), BF),
            pltpu.VMEM((3, 8, 4, 32, WIDTH), BF),
            pltpu.VMEM((ROWS, HD), F32),
            pltpu.VMEM((ROWS, HD), F32),
            pltpu.VMEM((1, 3072), F32),
            pltpu.VMEM((1, 3072), F32),
            pltpu.VMEM((1, WIDTH), F32),
            pltpu.VMEM((1, HD), F32),
            pltpu.VMEM((1, HD), F32),
            pltpu.VMEM((1, HD), F32),
            pltpu.VMEM((3, ROWS, HD), BF),
            pltpu.VMEM((3, 8, 2, ROWS // 2, 2 * HD), BF),
            pltpu.VMEM((3, ROWS, 8 * HD), BF),
            pltpu.VMEM((ROWS, WIDTH), F32),
            pltpu.VMEM((ROWS, HD), F32),
            pltpu.VMEM((ROWS, HD), F32),
            pltpu.VMEM((ROWS, HD), F32),
            pltpu.VMEM((ROWS, HD), jnp.int32),
            dma((15,)),
            dma((2, 4, 5, 3)),
            dma((64,)),
            dma((6, 4)),
            dma((6, 4)),
            dma((6, 4)),
            dma((6, 4)),
            dma((6, 8)),
            dma((6, 8)),
            dma((4,)),
            dma((4,)),
            dma((4,)),
            dma((4,)),
            dma((8,)),
            dma((8,)),
            dma((3,)),
            dma((3,)),
            dma((3, 7)),
            dma((3, 7)),
            dma((3, 7)),
            dma((3, 7)),
            dma((2, 8)),
            dma((2, 8)),
            dma((5, 8)),
            dma((5, 8)),
        ],
        compiler_params=pltpu.CompilerParams(
            collective_id=1, has_side_effects=True, vmem_limit_bytes=60 * 2**20
        ),
    )(
        video,
        text,
        w_qkv,
        w_out.reshape(3, 128, WIDTH),
        shift.reshape(1, -1),
        scale.reshape(1, -1),
        gate.reshape(1, -1),
        q_gain.reshape(1, HD),
        k_gain.reshape(1, HD),
        jnp.asarray(freqs),
        clip_lengths,
        text_owner,
    )


def solution(mesh):
    return jax.shard_map(
        on_device,
        mesh=mesh,
        in_specs=(
            P(("dp", "blk"), "head"),
            P(("dp", "blk"), "head"),
            P(),
            P(),
            P(),
            P("blk", "head"),
            P("head", "blk"),
            P(),
            P(),
            P("dp"),
            P("dp"),
        ),
        out_specs=(P(("dp", "blk"), "head"), P(("dp", "blk"), "head")),
        check_vma=False,
    )
```

time: 452 us -> 164 us (0.36)
  waiting for transfers between devices: 327 us -> 0 us
  Pallas kernels: 0 us -> 160 us
  matrix products: 55.2 us -> 0 us
  other arithmetic: 36.9 us -> 0 us
  local copies, waits for them, and re-layouts: 17.6 us -> 2.46 us
  between operations: 14.3 us -> 0.65 us
    all_gather x5 -> x0, waiting for transfers between devices: 239 us -> none  [the longest x1 78.5 us: on_device(): whole = lax.all_gather(local_tokens, 'head', axis=1, tiled=True)]
    pallas_call x0 -> x1, Pallas kernels: none -> 160 us  [on_device(): pl.pallas_call(sublayer_kernel, name='sublayer', out_shape=(jax.ShapeDtyp...]
    unnamed x7 -> x0, waiting for transfers between devices: 88.8 us -> none
    dot_general x4 -> x0, matrix products: 55.2 us -> none  [the longest x1 19.5 us: absorb(): jnp.einsum('qhd,khd->hqk', queries, key_part, preferred_element_type=jnp....]
    reduce_sum x10 -> x0, other arithmetic: 26.2 us -> none  [the longest x1 19 us: absorb(): totals = jnp.sum(weights, axis=-1)]
    unnamed x22 -> x4, local copies, waits for them, and re-layouts: 13.1 us -> 2.46 us
  transfers between devices with their start and end apart: 6 -> 0, of which waited for: 6 -> 0; matrix products, arithmetic and copies ran while one was open for 16% -> 0% of each run, Pallas kernels for 0% -> 0%
where the time goes in v2:
time: 164 us; the launch traced here: 163 us
  Pallas kernels  160 us (98%)
  local copies, waits for them, and re-layouts  2.46 us (2%)
    pallas_call x1, Pallas kernels, on_device(): pl.pallas_call(sublayer_kernel, name='sublayer', out_shape=(jax.ShapeDtyp...  160 us

profile of v2, /device:TPU:32, one launch (start us, length us, event | category | flops | bytes accessed | tf_op | source)
XLA Modules:
  0.0 163.2 jit_solution(15339439000876332681)
XLA Ops:
  0.6 160.1 %sublayer.1 = (bf16[512,384]{1,0:T(8,128)(2,1)}, bf16[128,384]{1,0:T(8,128)(2,1)}) custom-call(bf16[512,384]{1,0:T(8,128)(2,1)} %video.1, bf16[128,384]{1,0:T(8,128)(2,1)} %text.1, bf16[384,1152]{1,0:T(8,128)(2,1)} %w_qkv.1, bf16[3,128,384]{2,1,0:T(8,128)(2,1)} %bitcast.6, f32[1,3072]{1,0:T(1,128)} %bitcast.7, f32[1,3072]{1,0:T(1,128)} %bitcast.8, ...), custom_call_target="tpu_custom_call" | custom-call | tf_op jit(solution)/shard_map/sublayer/pallas_call | solution.py:583
  160.8 0.0 copy-start
  160.8 1.8 %copy.16 = bf16[512,384]{1,0:T(8,128)(2,1)} copy(bf16[512,384]{1,0:T(8,128)(2,1)} %get-tuple-element.4) | data formatting | bytes 786432
  162.6 0.0 copy-done
  162.6 0.6 copy.17
Async XLA Ops:
  160.8 1.8 %copy-start = (bf16[128,384]{1,0:T(8,128)(2,1)S(1)}, bf16[128,384]{1,0:T(8,128)(2,1)}, u32[]{:S(2)}) copy-start(bf16[128,384]{1,0:T(8,128)(2,1)} %get-tuple-element.5) | copy-start | bytes 294916

commit v3 on v2

--- a/solution.py
+++ b/solution.py
@@ -37,7 +37,15 @@
     pl.semaphore_wait(barrier, len(devices))
 
 
-PARTS = {"all": (0, 128, 0), "a": (0, 64, 0), "b": (64, 64, 1), "a0": (0, 32, 0), "a1": (32, 32, 2)}
+PARTS = {
+    "all": (0, 128, 0),
+    "f0": (0, 64, 0),
+    "f1": (64, 64, 1),
+    "a": (0, 96, 0),
+    "b": (96, 32, 1),
+    "a0": (0, 48, 0),
+    "a1": (48, 48, 2),
+}
 
 
 def sublayer_kernel(
@@ -69,6 +77,7 @@
     q_gain,
     k_gain,
     freqs,
+    q_block,
     q,
     kvbuf,
     att,
@@ -86,6 +95,8 @@
     wl_send,
     sib_recv,
     sib_send,
+    q_recv,
+    q_send,
     ol_recv,
     or_recv,
     or_send,
@@ -159,7 +170,7 @@
         tok_wait(1, 0, t, "all")
         tok_pass(slot[1][0], t, "a", 1, 3, right)
         tok_pass(slot[1][0], t, "a", 1, 1, left)
-        for dx, part, device in ((3, "a", right), (1, "b", left)):
+        for dx, part, device in ((3, "f0", right), (1, "f1", left)):
             tok_wait(0, dx, t, "all")
             tok_pass(slot[0][dx], t, part, 0, 2, device)
             tok_pass(slot[0][dx], t, "b", 1, dx, over)
@@ -168,8 +179,8 @@
         for dx, part, device in ((3, "a0", right), (1, "a1", left)):
             tok_wait(1, dx, t, "a")
             tok_pass(slot[1][dx], t, part, 1, 2, device)
-        tok_wait(0, 2, t, "a")
-        tok_wait(0, 2, t, "b")
+        tok_wait(0, 2, t, "f0")
+        tok_wait(0, 2, t, "f1")
         tok_pass(slot[0][2], t, "b", 1, 2, over)
 
     def stage3(t):
@@ -192,7 +203,7 @@
         first, count = (0, 192) if half is None else (half * 96, 96)
         side = core if side is None else side
         rows = pl.ds(pl.multiple_of(block * WIDTH + side * 192 + first, 32), count)
-        return wkv.at[rows, pl.ds(256 * p, 256)] if p < 3 else wq.at[rows, pl.ds(128 * p - 384, 128)]
+        return wkv.at[rows, pl.ds(256 * p, 256)]
 
     def w_cols(p):
         return pl.ds(384 * p + 128, 256) if p < 3 else pl.ds(384 * (p - 3), 128)
@@ -225,6 +236,43 @@
                 ref = w_at(block, p, i if s == 4 else None, 1 - core)
                 landed(ref, sib_recv.at[p, 2 * (s - 1) + i])
 
+    def q_at(block, half, quarter):
+        part = wq.at[block, quarter]
+        return part if half is None else part.at[pl.ds(half * 48, 48)]
+
+    def q_pair(s, quarter, split):
+        lo, hi = lax.rem(z + 8 - s, 8), lax.rem(z + s, 8)
+        return q_at(lo, 0 if split else None, quarter), q_at(hi, 1 if split else None, quarter)
+
+    def q_sends(s):
+        a, b = q_pair(s, dp, s == 3)
+        send(remote(a, a, wr_send.at[3, s], wl_recv.at[3, s], up))
+        send(remote(b, b, wl_send.at[3, s], wr_recv.at[3, s], down))
+
+    def q_step(s):
+        a, b = q_pair(s, dp, s == 4)
+        landed(a, wl_recv.at[3, s - 1])
+        landed(b, wr_recv.at[3, s - 1])
+        if s < 4:
+            q_sends(s)
+        for i in range(2):
+            for k, ref in enumerate((a, b)):
+                n = 2 * (s - 1) + k
+                send(remote(ref, ref, q_send.at[i, n], q_recv.at[i, n], mates[i]))
+
+    def q_on():
+        for s in range(1, 5):
+            for k, ref in enumerate(q_pair(s, mates[1][0], s == 4)):
+                landed(ref, q_recv.at[1, 2 * (s - 1) + k])
+        part = wq.at[:, mates[1][0]]
+        send(remote(part, part, q_send.at[2, 0], q_recv.at[2, 0], sibling))
+
+    def q_wait():
+        for s in range(1, 5):
+            for k, ref in enumerate(q_pair(s, sibling[0], s == 4)):
+                landed(ref, q_recv.at[0, 2 * (s - 1) + k])
+        landed(wq.at[:, mates[2][0]], q_recv.at[2, 0])
+
     quarter = w_out.at[:, pl.ds(pl.multiple_of(dp * 32, 32), 32)]
 
     def out_first():
@@ -290,12 +338,26 @@
         pltpu.make_async_copy(quarter, ring.at[z], local_sem.at[2]),
     ]
     block_rows = pl.ds(pl.multiple_of(z * WIDTH, WIDTH), WIDTH)
-    for p in range(6):
-        target = wkv.at[:, pl.ds(256 * p, 256)] if p < 3 else wq.at[:, pl.ds(128 * p - 384, 128)]
+    own_queries, own_quarters = [], []
+    for p in range(3):
         own.append(
             pltpu.make_async_copy(
-                w_qkv.at[:, w_cols(p)], target.at[block_rows], local_sem.at[3 + p]
+                w_qkv.at[:, w_cols(p)],
+                wkv.at[block_rows, pl.ds(256 * p, 256)],
+                local_sem.at[3 + p],
             )
+        )
+        own_queries.append(
+            pltpu.make_async_copy(
+                w_qkv.at[:, w_cols(3 + p)],
+                q_block.at[:, pl.ds(128 * p, 128)],
+                local_sem.at[6 + p],
+            )
+        )
+    for i, quarter_of in enumerate((dp, mates[0][0], mates[1][0])):
+        rows = pl.ds(pl.multiple_of(quarter_of * 96, 96), 96)
+        own_quarters.append(
+            pltpu.make_async_copy(q_block.at[rows], wq.at[z, quarter_of], local_sem.at[15 + i])
         )
     small = [
         pltpu.make_async_copy(a, b, local_sem.at[9 + i])
@@ -310,15 +372,21 @@
             )
         )
     ]
-    for p in range(6):
+    for copy in own_queries:
+        copy.start()
+    for p in range(3):
         ring_first(p)
-    out_first()
-    for t in range(3):
+    for t in range(5):
         stage0(t)
     for copy in small + own:
         copy.start()
     for copy in small:
         copy.wait()
+
+    def query_first():
+        src = q_block.at[pl.ds(pl.multiple_of(dp * 96, 96), 96)]
+        send(remote(src, wq.at[z, dp], wr_send.at[3, 0], wl_recv.at[3, 0], up))
+        send(remote(src, wq.at[z, dp], wl_send.at[3, 0], wr_recv.at[3, 0], down))
 
     e0 = lengths[0]
     e1 = e0 + lengths[1]
@@ -354,43 +422,40 @@
 
     def ring_steps(s, *pieces):
         for p in pieces:
-            if p == 6:
+            if p == 4:
                 out_step(s)
+            elif p == 3:
+                q_step(s)
             else:
                 ring_step(p, s)
 
-    tables(0)
-    stage1(0)
-    stage0(3)
-    ring_steps(1, 0, 1)
-    tables(1)
-    stage1(1)
-    stage2(0)
-    stage0(4)
-    ring_steps(1, 2, 3)
-    tables(2)
-    for copy in own:
+    for t in range(5):
+        tables(t)
+        stage1(t)
+        if t < 3:
+            ring_steps(1, t)
+    for copy in own_queries:
         copy.wait()
-    stage1(2)
-    stage2(1)
-    ring_steps(1, 4, 5, 6)
+    for copy in own_quarters:
+        copy.start()
+    query_first()
+    out_first()
+    for t in range(5):
+        stage2(t)
+        if t < 3:
+            ring_steps(2, t)
+    for copy in own + own_quarters:
+        copy.wait()
+    ring_steps(1, 3, 4)
     stage3(0)
-    tables(3)
-    stage1(3)
-    stage2(2)
-    ring_steps(2, 0, 1, 2)
+    ring_steps(3, 0, 1, 2)
     stage3(1)
-    tables(4)
-    stage1(4)
-    stage2(3)
-    ring_steps(2, 3, 4, 5, 6)
+    ring_steps(2, 3, 4)
     stage3(2)
-    stage2(4)
-    ring_steps(3, 0, 1, 2)
+    ring_steps(4, 0, 1, 2)
+    ring_steps(3, 3, 4)
     stage3(3)
-    ring_steps(3, 3, 4, 5, 6)
     stage3(4)
-    ring_steps(4, 0, 1, 2)
     sib_wait(0)
 
     def own_sends(h):
@@ -429,15 +494,17 @@
             kvbuf[h, z, i, :, HD : 2 * HD] = values[rows]
         if h == 0:
             own_sends(0)
-            ring_steps(4, 3, 4, 5, 6)
+            ring_steps(4, 3, 4)
+            q_on()
             swap()
             sib_wait(1)
             sib_wait(2)
-        else:
-            pass_on(0, h - 1)
-    for p in range(3, 6):
-        sib_wait(p)
-    queries = jnp.dot(mod[...], wq[...], preferred_element_type=F32)
+        elif h == 1:
+            own_sends(1)
+            pass_on(0, 0)
+    q_wait()
+    pass_on(0, 1)
+    queries = jnp.dot(mod[...], wq[...].reshape(3072, WIDTH), preferred_element_type=F32)
     for h in range(3):
         q[h] = rms_rope(queries[:, h * HD : (h + 1) * HD], q_gain[...]).astype(BF)
     proj[...] = jnp.zeros_like(proj)
@@ -450,17 +517,22 @@
         values = kvbuf[h, b, :, :, HD : 2 * HD].reshape(ROWS, HD)
         column = lax.broadcasted_iota(jnp.int32, (1, ROWS), 1)
         key_clip = clips(b * VROWS + column, column < VROWS, owners[b // 2])
-        for t in range(5):
-            rows = pl.ds(t * TILE, TILE)
-            scores = lax.dot_general(
+        tiles = [pl.ds(t * TILE, TILE) for t in range(5)]
+        scored = [
+            lax.dot_general(
                 q[h, rows, :], keys, (((1,), (1,)), ((), ())), preferred_element_type=F32
             )
+            for rows in tiles
+        ]
+        weighed = []
+        for rows, scores in zip(tiles, scored):
             scores = jnp.where(q_clip[rows, 0:1] == key_clip, scores, -1e30)
             old = jnp.where(first, -1e30, best[rows, 0:1])
             newest = jnp.maximum(old, jnp.max(scores, axis=1, keepdims=True))
             weights = jnp.exp2((scores - newest) * factor)
-            keep = jnp.exp2((old - newest) * factor)
             best[rows, :] = jnp.broadcast_to(newest, (TILE, HD))
+            weighed.append((weights, jnp.exp2((old - newest) * factor)))
+        for t, (rows, (weights, keep)) in enumerate(zip(tiles, weighed)):
             count = jnp.sum(weights, axis=1, keepdims=True)
             summed = jnp.dot(weights.astype(BF), values, preferred_element_type=F32)
             prior = jnp.where(first, 0.0, total[rows, 0:1])
@@ -505,9 +577,9 @@
         def _():
             pass_on(h, j)
 
-        @pl.when((j == 1) & (h < 2))
-        def _():
-            own_sends(h + 1)
+        @pl.when(t == 4)
+        def _():
+            own_sends(2)
 
         @pl.when(t == 1)
         def _():
@@ -517,13 +589,16 @@
         def _():
             share_on()
 
-        @pl.when((j == 0) & (h > 0))
-        def _():
-            unit(h - 1, lax.rem(z + 4, 8), False)
-            finish(h - 1)
-
-        away = (j + 1) // 2
+        away = jnp.where(j == 6, 4, (j + 1) // 2)
         unit(h, lax.rem(jnp.where(odd == 1, z + 8 - away, z + away), 8), j == 0)
+
+        @pl.when(j == 5)
+        def _():
+            unit(h, lax.rem(z + 3, 8), False)
+
+        @pl.when(j == 6)
+        def _():
+            finish(h)
 
         @pl.when(t == 17)
         def _():
@@ -536,7 +611,8 @@
 
         return carry
 
-    lax.fori_loop(0, 21, step, 0)
+    lax.fori_loop(0, 20, step, 0)
+    pass_on(2, 6)
     unit(2, lax.rem(z + 4, 8), False, finish_tile)
     weights_out = wo[2].reshape(8 * HD, WIDTH)
     for t in range(5):
@@ -593,7 +669,7 @@
             pltpu.VMEM((ROWS, 3072), BF),
             pltpu.VMEM((ROWS, 3072), BF),
             pltpu.VMEM((3072, 768), BF),
-            pltpu.VMEM((3072, 384), BF),
+            pltpu.VMEM((8, 4, 96, WIDTH), BF),
             pltpu.VMEM((8, 3, 32, WIDTH), BF),
             pltpu.VMEM((3, 8, 4, 32, WIDTH), BF),
             pltpu.VMEM((ROWS, HD), F32),
@@ -604,6 +680,7 @@
             pltpu.VMEM((1, HD), F32),
             pltpu.VMEM((1, HD), F32),
             pltpu.VMEM((1, HD), F32),
+            pltpu.VMEM((WIDTH, WIDTH), BF),
             pltpu.VMEM((3, ROWS, HD), BF),
             pltpu.VMEM((3, 8, 2, ROWS // 2, 2 * HD), BF),
             pltpu.VMEM((3, ROWS, 8 * HD), BF),
@@ -612,15 +689,17 @@
             pltpu.VMEM((ROWS, HD), F32),
             pltpu.VMEM((ROWS, HD), F32),
             pltpu.VMEM((ROWS, HD), jnp.int32),
-            dma((15,)),
+            dma((18,)),
             dma((2, 4, 5, 3)),
             dma((64,)),
-            dma((6, 4)),
-            dma((6, 4)),
-            dma((6, 4)),
-            dma((6, 4)),
-            dma((6, 8)),
-            dma((6, 8)),
+            dma((4, 4)),
+            dma((4, 4)),
+            dma((4, 4)),
+            dma((4, 4)),
+            dma((3, 8)),
+            dma((3, 8)),
+            dma((3, 8)),
+            dma((3, 8)),
             dma((4,)),
             dma((4,)),
             dma((4,)),

time: 164 us -> 154 us (0.939)
  Pallas kernels: 160 us -> 150 us
    pallas_call x1, Pallas kernels: 160 us -> 150 us  [on_device(): pl.pallas_call(sublayer_kernel, name='sublayer', out_shape=(jax.ShapeDtyp...]
where the time goes in v3:
time: 154 us; the launch traced here: 153 us
  Pallas kernels  150 us (97%)
  local copies, waits for them, and re-layouts  2.46 us (2%)
    pallas_call x1, Pallas kernels, on_device(): pl.pallas_call(sublayer_kernel, name='sublayer', out_shape=(jax.ShapeDtyp...  150 us

profile of v3, /device:TPU:32, one launch (start us, length us, event | category | flops | bytes accessed | tf_op | source)
XLA Modules:
  0.0 152.9 jit_solution(7363444511012688424)
XLA Ops:
  0.6 149.8 %sublayer.1 = (bf16[512,384]{1,0:T(8,128)(2,1)}, bf16[128,384]{1,0:T(8,128)(2,1)}) custom-call(bf16[512,384]{1,0:T(8,128)(2,1)} %video.1, bf16[128,384]{1,0:T(8,128)(2,1)} %text.1, bf16[384,1152]{1,0:T(8,128)(2,1)} %w_qkv.1, bf16[3,128,384]{2,1,0:T(8,128)(2,1)} %bitcast.6, f32[1,3072]{1,0:T(1,128)} %bitcast.7, f32[1,3072]{1,0:T(1,128)} %bitcast.8, ...), custom_call_target="tpu_custom_call" | custom-call | tf_op jit(solution)/shard_map/sublayer/pallas_call | solution.py:659
  150.4 0.0 copy-start
  150.4 1.8 %copy.16 = bf16[512,384]{1,0:T(8,128)(2,1)} copy(bf16[512,384]{1,0:T(8,128)(2,1)} %get-tuple-element.4) | data formatting | bytes 786432
  152.2 0.0 copy-done
  152.2 0.6 copy.17
Async XLA Ops:
  150.4 1.8 %copy-start = (bf16[128,384]{1,0:T(8,128)(2,1)S(1)}, bf16[128,384]{1,0:T(8,128)(2,1)}, u32[]{:S(2)}) copy-start(bf16[128,384]{1,0:T(8,128)(2,1)} %get-tuple-element.5) | copy-start | bytes 294916

commit v4 on v3

--- a/solution.py
+++ b/solution.py
@@ -189,7 +189,7 @@
         normalise(t)
 
     def normalise(t):
-        @pl.loop(0, 8)
+        @pl.loop(0, 8, unroll=4)
         def _(i):
             rows = pl.ds(pl.multiple_of(t * TILE + i * 16, 16), 16)
             value = tok[rows, :].astype(F32)

time: 154 us -> 150 us (0.974)
  Pallas kernels: 150 us -> 147 us
    pallas_call x1, Pallas kernels: 150 us -> 147 us  [on_device(): pl.pallas_call(sublayer_kernel, name='sublayer', out_shape=(jax.ShapeDtyp...]
where the time goes in v4:
time: 150 us
  Pallas kernels  147 us (98%)
  local copies, waits for them, and re-layouts  2.46 us (2%)
    pallas_call x1, Pallas kernels, on_device(): pl.pallas_call(sublayer_kernel, name='sublayer', out_shape=(jax.ShapeDtyp...  147 us

profile of v4, /device:TPU:32, one launch (start us, length us, event | category | flops | bytes accessed | tf_op | source)
XLA Modules:
  0.0 149.7 jit_solution(5406960060462335444)
XLA Ops:
  0.6 146.6 %sublayer.1 = (bf16[512,384]{1,0:T(8,128)(2,1)}, bf16[128,384]{1,0:T(8,128)(2,1)}) custom-call(bf16[512,384]{1,0:T(8,128)(2,1)} %video.1, bf16[128,384]{1,0:T(8,128)(2,1)} %text.1, bf16[384,1152]{1,0:T(8,128)(2,1)} %w_qkv.1, bf16[3,128,384]{2,1,0:T(8,128)(2,1)} %bitcast.6, f32[1,3072]{1,0:T(1,128)} %bitcast.7, f32[1,3072]{1,0:T(1,128)} %bitcast.8, ...), custom_call_target="tpu_custom_call" | custom-call | tf_op jit(solution)/shard_map/sublayer/pallas_call | solution.py:659
  147.2 0.0 copy-start
  147.2 1.8 %copy.16 = bf16[512,384]{1,0:T(8,128)(2,1)} copy(bf16[512,384]{1,0:T(8,128)(2,1)} %get-tuple-element.4) | data formatting | bytes 786432
  149.0 0.0 copy-done
  149.0 0.6 copy.17
Async XLA Ops:
  147.2 1.8 %copy-start = (bf16[128,384]{1,0:T(8,128)(2,1)S(1)}, bf16[128,384]{1,0:T(8,128)(2,1)}, u32[]{:S(2)}) copy-start(bf16[128,384]{1,0:T(8,128)(2,1)} %get-tuple-element.5) | copy-start | bytes 294916

commit v5 on v4

--- a/solution.py
+++ b/solution.py
@@ -41,10 +41,10 @@
     "all": (0, 128, 0),
     "f0": (0, 64, 0),
     "f1": (64, 64, 1),
-    "a": (0, 96, 0),
-    "b": (96, 32, 1),
+    "a": (0, 80, 0),
+    "b": (80, 48, 1),
     "a0": (0, 48, 0),
-    "a1": (48, 48, 2),
+    "a1": (48, 32, 2),
 }
 
 
@@ -518,28 +518,35 @@
         column = lax.broadcasted_iota(jnp.int32, (1, ROWS), 1)
         key_clip = clips(b * VROWS + column, column < VROWS, owners[b // 2])
         tiles = [pl.ds(t * TILE, TILE) for t in range(5)]
-        scored = [
-            lax.dot_general(
+
+        def score(rows):
+            return lax.dot_general(
                 q[h, rows, :], keys, (((1,), (1,)), ((), ())), preferred_element_type=F32
             )
-            for rows in tiles
-        ]
-        weighed = []
-        for rows, scores in zip(tiles, scored):
+
+        def weigh(rows, scores):
             scores = jnp.where(q_clip[rows, 0:1] == key_clip, scores, -1e30)
             old = jnp.where(first, -1e30, best[rows, 0:1])
             newest = jnp.maximum(old, jnp.max(scores, axis=1, keepdims=True))
-            weights = jnp.exp2((scores - newest) * factor)
             best[rows, :] = jnp.broadcast_to(newest, (TILE, HD))
-            weighed.append((weights, jnp.exp2((old - newest) * factor)))
-        for t, (rows, (weights, keep)) in enumerate(zip(tiles, weighed)):
+            return jnp.exp2((scores - newest) * factor), jnp.exp2((old - newest) * factor)
+
+        def absorb(rows, weights, keep):
             count = jnp.sum(weights, axis=1, keepdims=True)
             summed = jnp.dot(weights.astype(BF), values, preferred_element_type=F32)
             prior = jnp.where(first, 0.0, total[rows, 0:1])
             before = jnp.where(first, 0.0, acc[rows, :])
             total[rows, :] = jnp.broadcast_to(prior * keep + count, (TILE, HD))
             acc[rows, :] = before * keep + summed
-            if each is not None:
+
+        scored = [score(rows) for rows in tiles]
+        if each is None:
+            weighed = [weigh(rows, scores) for rows, scores in zip(tiles, scored)]
+            for rows, pair in zip(tiles, weighed):
+                absorb(rows, *pair)
+        else:
+            for t, rows in enumerate(tiles):
+                absorb(rows, *weigh(rows, scored[t]))
                 each(t)
 
     def att_copy(h, d):

time: 150 us -> 148 us (0.987)
  Pallas kernels: 147 us -> 145 us
    pallas_call x1, Pallas kernels: 147 us -> 145 us  [on_device(): pl.pallas_call(sublayer_kernel, name='sublayer', out_shape=(jax.ShapeDtyp...]
where the time goes in v5:
time: 148 us
  Pallas kernels  145 us (98%)
  local copies, waits for them, and re-layouts  2.46 us (2%)
    pallas_call x1, Pallas kernels, on_device(): pl.pallas_call(sublayer_kernel, name='sublayer', out_shape=(jax.ShapeDtyp...  145 us

profile of v5, /device:TPU:32, one launch (start us, length us, event | category | flops | bytes accessed | tf_op | source)
XLA Modules:
  0.0 148.0 jit_solution(17969557554398647049)
XLA Ops:
  0.6 144.9 %sublayer.1 = (bf16[512,384]{1,0:T(8,128)(2,1)}, bf16[128,384]{1,0:T(8,128)(2,1)}) custom-call(bf16[512,384]{1,0:T(8,128)(2,1)} %video.1, bf16[128,384]{1,0:T(8,128)(2,1)} %text.1, bf16[384,1152]{1,0:T(8,128)(2,1)} %w_qkv.1, bf16[3,128,384]{2,1,0:T(8,128)(2,1)} %bitcast.6, f32[1,3072]{1,0:T(1,128)} %bitcast.7, f32[1,3072]{1,0:T(1,128)} %bitcast.8, ...), custom_call_target="tpu_custom_call" | custom-call | tf_op jit(solution)/shard_map/sublayer/pallas_call | solution.py:666
  145.6 0.0 copy-start
  145.6 1.8 %copy.16 = bf16[512,384]{1,0:T(8,128)(2,1)} copy(bf16[512,384]{1,0:T(8,128)(2,1)} %get-tuple-element.4) | data formatting | bytes 786432
  147.4 0.0 copy-done
  147.4 0.6 copy.17
Async XLA Ops:
  145.6 1.8 %copy-start = (bf16[128,384]{1,0:T(8,128)(2,1)S(1)}, bf16[128,384]{1,0:T(8,128)(2,1)}, u32[]{:S(2)}) copy-start(bf16[128,384]{1,0:T(8,128)(2,1)} %get-tuple-element.5) | copy-start | bytes 294916

commit v6 on v5

--- a/solution.py
+++ b/solution.py
@@ -573,8 +573,16 @@
     def finish_tile(t):
         rows = pl.ds(t * TILE, TILE)
         att[2, rows, mine] = (acc[rows, :] / total[rows, :]).astype(BF)
-        for d in range(1, 8):
-            last_copy(t, d).start()
+        for flip, dx in ((1, 2), (1, 1), (1, 3), (0, 2), (1, 0), (0, 1), (0, 3)):
+            target = slot[flip][dx]
+            d = lax.rem(target - head + 8, 8)
+            remote(
+                att.at[2, rows, mine],
+                att.at[2, rows, mine],
+                last_send.at[t, d],
+                last_recv.at[t, 8 - d],
+                (dp, z, target),
+            ).start()
 
     def step(t, carry):
         h, j = t // 7, lax.rem(t, 7)

time: 148 us -> 148 us (level)
  no operation moved by 1% of the time
where the time goes in v6:
time: 148 us
  Pallas kernels  145 us (98%)
  local copies, waits for them, and re-layouts  2.46 us (2%)
    pallas_call x1, Pallas kernels, on_device(): pl.pallas_call(sublayer_kernel, name='sublayer', out_shape=(jax.ShapeDtyp...  145 us

profile of v6, /device:TPU:32, one launch (start us, length us, event | category | flops | bytes accessed | tf_op | source)
XLA Modules:
  0.0 147.7 jit_solution(16604796756317027231)
XLA Ops:
  0.6 144.6 %sublayer.1 = (bf16[512,384]{1,0:T(8,128)(2,1)}, bf16[128,384]{1,0:T(8,128)(2,1)}) custom-call(bf16[512,384]{1,0:T(8,128)(2,1)} %video.1, bf16[128,384]{1,0:T(8,128)(2,1)} %text.1, bf16[384,1152]{1,0:T(8,128)(2,1)} %w_qkv.1, bf16[3,128,384]{2,1,0:T(8,128)(2,1)} %bitcast.6, f32[1,3072]{1,0:T(1,128)} %bitcast.7, f32[1,3072]{1,0:T(1,128)} %bitcast.8, ...), custom_call_target="tpu_custom_call" | custom-call | tf_op jit(solution)/shard_map/sublayer/pallas_call | solution.py:674
  145.2 0.0 copy-start
  145.2 1.8 %copy.16 = bf16[512,384]{1,0:T(8,128)(2,1)} copy(bf16[512,384]{1,0:T(8,128)(2,1)} %get-tuple-element.4) | data formatting | bytes 786432
  147.0 0.0 copy-done
  147.0 0.6 copy.17
Async XLA Ops:
  145.2 1.8 %copy-start = (bf16[128,384]{1,0:T(8,128)(2,1)S(1)}, bf16[128,384]{1,0:T(8,128)(2,1)}, u32[]{:S(2)}) copy-start(bf16[128,384]{1,0:T(8,128)(2,1)} %get-tuple-element.5) | copy-start | bytes 294916
